TPU v7x, 32 devices: a whole 2x2x4 slice. The times are simulated.
32 devices in a mesh: slab: 16 (over z, y, core), tm: 2 (over x).
Axes of the slice: x: 2, y: 2, z: 4, core: 2. Of those that a mesh axis runs over, the one named last changes fastest.
Arguments:
- recording: bfloat16 [512, 32768], P('tm', 'slab'), may hold values from -6 to 6
- footprints: bfloat16 [2176, 4096], P(None, 'slab'), may hold values from -0.125 to 0.125
- traces: float32 [512, 4096], P('tm', 'slab'), may hold values from 0 to 2
- live_count: int32 [16], replicated, may hold values from 1 to 256, 3072 in all
Outputs:
- new_traces: float32 [512, 4096], P('tm', 'slab')
- new_footprints: bfloat16 [2176, 4096], P('tm', 'slab')
Inputs may be any that keep to these rules, and one draw needn't show every extreme that they name: Slots 0 .. live_count[s] - 1 of slab s are live; some slab has all 256 live.
All inputs are finite; a program needn't handle non-finite values.
Results may differ from a plain program's by a relative error of at most 0.0034.
Values may be sent and summed in bfloat16 or wider, within the bound.
No kernel may reach another device: no remote copies, remote signals or barrier semaphores. Data moves between devices by JAX's collectives and lax.ppermute only.
A program may use at most 64 MiB of HBM per device.

v0:
```python
import functools

import jax
import jax.numpy as jnp
from jax import lax
from jax.experimental import pallas as pl
from jax.experimental.pallas import tpu as pltpu
from jax.sharding import PartitionSpec as P

GROUP = 128
BF = jnp.bfloat16
F32 = jnp.float32
WHOLE = pl.BlockSpec(memory_space=pltpu.VMEM)
LEFT_THERE = pl.BlockSpec(memory_space=pl.ANY)
COPIES = pltpu.SemaphoreType.DMA
shape = jax.ShapeDtypeStruct


def mm(left, right):
    return jnp.dot(left, right, preferred_element_type=F32)


def mm_t(left, right):
    return lax.dot_general(left, right, (((1,), (1,)), ((), ())), preferred_element_type=F32)


def t_mm(left, right):
    return lax.dot_general(left, right, (((0,), (0,)), ((), ())), preferred_element_type=F32)


def halves(wide):
    high = wide.astype(BF)
    return high, (wide - high.astype(F32)).astype(BF)


def living(count, block):
    slots = lax.broadcasted_iota(jnp.int32, block.shape, 1)
    return jnp.where(slots < count, block, jnp.zeros_like(block))


def diagonal(square):
    rows = lax.broadcasted_iota(jnp.int32, square.shape, 0)
    columns = lax.broadcasted_iota(jnp.int32, square.shape, 1)
    return jnp.sum(jnp.where(rows == columns, square, 0.0), axis=0, keepdims=True)


def at_end(axis):
    return lax.axis_index(axis) == lax.axis_size(axis) - 1


def odd_slab():
    return lax.axis_index("slab") % 2 == 1


def call(body, outs, in_specs, out_specs, expected, **more):
    return pl.pallas_call(
        body,
        out_shape=outs,
        in_specs=in_specs,
        out_specs=out_specs,
        compiler_params=pltpu.CompilerParams(vmem_limit_bytes=32 * 1024 * 1024),
        cost_estimate=pl.CostEstimate(
            flops=0, bytes_accessed=int(expected * 3_690_000), transcendentals=0
        ),
        **more,
    )


def copied(source, target, sem):
    copy = pltpu.make_async_copy(source, target, sem)
    copy.start()
    return copy


def first_column(which, voxels, rim):
    return pl.multiple_of(rim + which * (voxels // 2), 128)


def rolled(block):
    half = block.shape[1] // 2
    return jnp.concatenate([block[:, half:], block[:, :half]], axis=1)


def packed(which, middle):
    frames = middle.shape[0] // 2
    top, bottom = middle[:frames], middle[frames:]
    low = jnp.where(which == 0, top, rolled(top))
    high = jnp.where(which == 0, rolled(bottom), bottom)
    slots = lax.broadcasted_iota(jnp.int32, low.shape, 1)
    return jnp.where(slots < low.shape[1] // 2, low, high)


def unpacked(which, block):
    turned = rolled(block)
    top = jnp.where(which == 0, block, turned)
    bottom = jnp.where(which == 0, turned, block)
    return jnp.concatenate([top, bottom], axis=0)


def for_near_and_far(forward, backward):
    odd = odd_slab()
    return jnp.where(odd, backward, forward), jnp.where(odd, forward, backward)


def from_prev_and_next(near, far):
    odd = odd_slab()
    return jnp.where(odd, near, far), jnp.where(odd, far, near)


def rim_kernel(voxels, live, movie, foot, start, far, near, count, *rest):
    numbers, head, tail, traces, edge, middle, sems = rest[-7:]
    rim = head.shape[0]
    frames = edge.shape[0]
    there = 1 - lax.axis_index("tm")
    small = [
        copied(live, numbers, sems.at[0]),
        copied(start, traces, sems.at[1]),
        copied(foot.at[pl.ds(0, rim)], head, sems.at[2]),
        copied(foot.at[pl.ds(voxels, rim)], tail, sems.at[3]),
        copied(movie.at[:, pl.ds(0, rim)], edge, sems.at[4]),
        copied(movie.at[:, pl.ds(voxels // 2, rim)], middle, sems.at[5]),
    ]
    large = []
    if len(rest) > 7:
        first = first_column(there, voxels, rim)
        for i in range(voxels // 2 // rim - 1):
            column = movie.at[:, pl.ds(pl.multiple_of(first + i * rim, 128), rim)]
            large.append(copied(column, rest[0].at[pl.ds(i * frames, frames)], sems.at[6 + i]))
    for copy in small:
        copy.wait()
    alive = numbers[lax.axis_index("slab")]
    count[...] = jnp.full(count.shape, alive, jnp.int32)
    high, low = halves(living(alive, traces[...]))
    ends = jnp.where(at_end("slab"), jnp.zeros_like(tail[...]), tail[...])
    forward = mm_t(high, ends) + mm_t(low, ends)
    backward = edge[...].astype(F32) - (mm_t(high, head[...]) + mm_t(low, head[...]))
    one, two = for_near_and_far(forward, backward)
    near[...] = one.astype(BF)
    far[...] = two.astype(BF)
    if large:
        rest[0][(voxels // 2 // rim - 1) * frames:] = packed(there, middle[...])
    for copy in large:
        copy.wait()


def drive_kernel(voxels, count, movie, foot, start, plan, scale, cross_high, cross_low, rims, flat, masked):
    rim = foot.shape[0] - voxels
    alive = count[0:1]
    masked[:voxels] = living(alive, foot[:voxels])
    ends = living(alive, foot[voxels:])
    masked[voxels:] = jnp.where(at_end("slab"), jnp.zeros_like(ends), ends)
    rims[:rim] = -masked[:rim]
    rims[rim:] = masked[voxels:]
    flat[...] = movie[:, :rim].T
    drive = mm(movie[...], masked[:voxels])
    gram = t_mm(masked[...], masked[...])
    inverse = 1.0 / (diagonal(gram) + 1e-06)
    scale[...] = jnp.broadcast_to(inverse, scale.shape)
    gram_high, gram_low = halves(gram)
    cross_high[...] = gram_high[:GROUP, GROUP:]
    cross_low[...] = gram_low[:GROUP, GROUP:]
    current = living(alive, start[...])
    high, low = halves(current)
    for at in range(0, current.shape[1], GROUP):
        columns = slice(at, at + GROUP)
        coupled = mm(high[:, at:], gram_high[at:, columns]) + mm(high[:, at:], gram_low[at:, columns])
        coupled = coupled + mm(low[:, at:], gram_high[at:, columns])
        plan[:, columns] = current[:, columns] + (drive[:, columns] - coupled) * inverse[:, columns]


def sweep_kernel(
    plan, scale, cross_high, cross_low, rims, flat, far, near, traces, rounded, far_next, near_next
):
    rim = flat.shape[0]
    edges = rims[...]
    beside = jnp.concatenate(from_prev_and_next(near[...], far[...]), axis=1)
    stepped = plan[...] + mm(beside, edges) * scale[0:1]
    first = jnp.maximum(stepped[:, :GROUP], 0.0)
    high, low = halves(first)
    cross = cross_high[...]
    coupled = mm(high, cross) + mm(high, cross_low[...]) + mm(low, cross)
    second = jnp.maximum(stepped[:, GROUP:] - coupled * scale[0:1, GROUP:], 0.0)
    whole = jnp.concatenate([high, second.astype(BF)], axis=1)
    rounded[...] = whole
    forward = mm_t(edges[rim:], whole)
    backward = flat[...].astype(F32) + mm_t(edges[:rim], whole)
    one, two = for_near_and_far(forward, backward)
    near_next[...] = one.astype(BF)
    far_next[...] = two.astype(BF)
    traces[:, :GROUP] = first
    traces[:, GROUP:] = second


def own_kernel(voxels, movie, foot, fit, flat, total, quad, rim_part):
    rim = flat.shape[0]
    main = voxels // 2 - rim
    traces = fit[...]
    square = t_mm(traces, traces)
    quad[...] = square
    high, low = halves(square)
    begins, ends = foot[:rim], foot[voxels:]
    rim_part[:rim] = mm(flat[...], traces) - (mm(begins, high) + mm(begins, low))
    rim_part[rim:] = -(mm(ends, high) + mm(ends, low))
    first = first_column(lax.axis_index("tm"), voxels, rim)
    total[:main] = t_mm(movie[:, pl.ds(first, main)], traces)
    total[main:] = t_mm(movie[:, voxels // 2:voxels // 2 + rim], traces)


def both_kernel(rim_part, fit, far, near, lead, sent):
    rim = lead.shape[0]
    first = lax.axis_index("tm") == 0
    before, after = from_prev_and_next(near[...], far[...])
    traces = fit[...]
    begins = rim_part[:rim] - mm(before, traces)
    ends = rim_part[rim:] + mm(after, traces)
    lead[...] = jnp.where(first, begins, ends)
    sent[...] = jnp.where(first, ends, begins).astype(BF)


def main_kernel(voxels, rim, foot, total, quad, movie, fit, traces, out, new_tr, scale, moved, sems):
    here = lax.axis_index("tm")
    frames = fit.shape[0]
    width = voxels // 2
    main = width - rim
    written = [copied(traces, new_tr, sems.at[0])]
    fitted = fit[...]
    square = quad[...] + t_mm(fitted, fitted)
    inverse = 1.0 / jnp.maximum(diagonal(square), 1.0)
    scale[...] = jnp.broadcast_to(inverse, scale.shape)
    high, low = halves(square)
    first = first_column(here, voxels, rim)
    row = pl.multiple_of(rim - here * (rim // 2), 64)
    for begin, end in ((0, width // 2), (width // 2, main), (main, width)):
        if begin < main:
            own = foot[pl.ds(pl.multiple_of(first + begin, 128), end - begin)]
            columns = range(begin // rim, end // rim)
            shown = jnp.concatenate([movie[i * frames:(i + 1) * frames] for i in columns], axis=1)
        else:
            own = foot[width:width + rim]
            shown = unpacked(here, movie[main // rim * frames:])
        part = total[begin:end] + t_mm(shown, fitted) - (mm(own, high) + mm(own, low))
        moved[begin:end] = jnp.maximum(own.astype(F32) + part * inverse, 0.0).astype(BF)
        if begin < main:
            target = out.at[pl.ds(row + begin, end - begin)]
            written.append(copied(moved.at[pl.ds(begin, end - begin)], target, sems.at[len(written)]))
        else:
            half = rim // 2
            source = moved.at[pl.ds(pl.multiple_of(main + here * half, 64), half)]
            target = out.at[pl.ds(pl.multiple_of((1 - here) * (out.shape[0] - half), 64), half)]
            written.append(copied(source, target, sems.at[len(written)]))
    for copy in written:
        copy.wait()


def edge_kernel(voxels, sofar, foot, lead, came, scale, out, moved, sem):
    rim = lead.shape[0]
    here = lax.axis_index("tm")
    own = foot[pl.ds(pl.multiple_of(here * voxels, 128), rim)].astype(F32)
    moved[...] = jnp.maximum(own + (lead[...] + came[...].astype(F32)) * scale[0:1], 0.0).astype(BF)
    row = pl.multiple_of(here * (out.shape[0] - rim), 64)
    copied(moved, out.at[pl.ds(row, rim)], sem).wait()


def swapped(block, first):
    route = [(i, i + 1) for i in range(first, lax.axis_size("slab") - 1, 2)]
    return lax.ppermute(block, "slab", route + [(j, i) for i, j in route])


def halved(voxels, rim, foot, recording, flat, outgoing, new_tr, rounded, far, near):
    frames = recording.shape[0]
    extended, neurons = foot.shape
    width, share = voxels // 2, extended // 2
    across = [(0, 1), (1, 0)]
    movie = lax.ppermute(outgoing, "tm", across)
    far = swapped(far, 1)
    near = swapped(near, 0)
    other = lax.ppermute(rounded, "tm", across)
    total, quad, rim_part = call(
        functools.partial(own_kernel, voxels),
        [
            shape((width, neurons), F32),
            shape((neurons, neurons), F32),
            shape((2 * rim, neurons), F32),
        ],
        [WHOLE] * 4,
        [WHOLE] * 3,
        0.6,
    )(recording, foot, rounded, flat)
    lead, sent = call(
        both_kernel,
        [shape((rim, neurons), F32), pltpu.VMEM((rim, neurons), BF)],
        [WHOLE] * 4,
        [WHOLE] * 2,
        0.3,
    )(rim_part, rounded, far, near)
    came = lax.ppermute(sent, "tm", across)
    sofar, new_tr, scale = call(
        functools.partial(main_kernel, voxels, rim),
        [pltpu.HBM((share, neurons), BF), pltpu.HBM((frames, neurons), F32), shape((8, neurons), F32)],
        [WHOLE] * 6,
        [LEFT_THERE] * 2 + [WHOLE],
        2.0,
        scratch_shapes=[pltpu.VMEM((width, neurons), BF), COPIES((4,))],
    )(foot, total, quad, movie, other, new_tr)
    new_foot = call(
        functools.partial(edge_kernel, voxels),
        pltpu.HBM((share, neurons), BF),
        [LEFT_THERE] + [WHOLE] * 4,
        LEFT_THERE,
        0.8,
        input_output_aliases={0: 0},
        scratch_shapes=[pltpu.VMEM((rim, neurons), BF), COPIES],
    )(sofar, foot, lead, came, scale)
    return new_tr, new_foot


def spread(voxels, rim, foot, recording, rounded):
    slabs, parts = lax.axis_size("slab"), lax.axis_size("tm")
    extended, neurons = foot.shape
    share = extended // parts
    here = lax.axis_index("tm")
    closing = here == parts - 1
    exact = lax.Precision.HIGHEST
    cut = voxels - (share - rim)
    columns = jnp.concatenate([recording[:, :cut], recording[:, :rim], recording[:, cut:]], 1)
    movie = lax.all_to_all(columns, "tm", split_axis=1, concat_axis=0, tiled=True)
    fit = lax.all_gather(rounded, "tm", axis=0, tiled=True)
    edge = jnp.where(here == 0, foot[voxels:], foot[:rim])
    seen = movie[:, :rim].astype(F32)
    sent = jnp.where(here == 0, 0.0, seen) - mm_t(fit, edge)
    ahead = [(i * parts, (i + 1) * parts) for i in range(slabs - 1)]
    behind = [((i + 2) * parts - 1, (i + 1) * parts - 1) for i in range(slabs - 1)]
    lead = jnp.where(closing, 0.0, seen) + lax.ppermute(sent, ("slab", "tm"), ahead + behind)
    lead = lax.dot_general(lead, fit.astype(F32), (((0,), (0,)), ((), ())), precision=exact)
    inner = t_mm(movie[:, rim:], fit)
    total = jnp.where(
        closing, jnp.concatenate([inner, lead], 0), jnp.concatenate([lead, inner], 0)
    )
    square = t_mm(fit, fit)
    own = lax.dynamic_slice_in_dim(foot, here * share, share, 0).astype(F32)
    total = total - jnp.dot(own, square, precision=exact)
    return jnp.maximum(own + total / jnp.maximum(jnp.diagonal(square), 1.0), 0.0).astype(BF)


def on_device(recording, footprints, traces, live_count):
    frames, voxels = recording.shape
    extended, neurons = footprints.shape
    rim = extended - voxels
    main = voxels // 2 // rim - 1
    split = lax.axis_size("tm") == 2
    share_shape = [pltpu.VMEM((main * frames + frames // 2, rim), BF)] if split else []
    pinned = [
        pltpu.with_memory_space_constraint(x, pltpu.HBM)
        for x in (live_count, recording, footprints, traces)
    ]
    far, near, count, *outgoing = call(
        functools.partial(rim_kernel, voxels),
        [
            pltpu.VMEM((frames, rim), BF),
            pltpu.VMEM((frames, rim), BF),
            pltpu.VMEM((8, neurons), jnp.int32),
        ]
        + share_shape,
        [LEFT_THERE] * 4,
        [WHOLE] * (3 + len(share_shape)),
        1.5,
        scratch_shapes=[
            pltpu.SMEM(live_count.shape, jnp.int32),
            pltpu.VMEM((rim, neurons), BF),
            pltpu.VMEM((rim, neurons), BF),
            pltpu.VMEM((frames, neurons), F32),
            pltpu.VMEM((frames, rim), BF),
            pltpu.VMEM((frames, rim), BF),
            COPIES((6 + main,)),
        ],
    )(*pinned)
    far = swapped(far, 1)
    near = swapped(near, 0)
    plan, scale, cross_high, cross_low, rims, flat, masked = call(
        functools.partial(drive_kernel, voxels),
        [
            shape((frames, neurons), F32),
            shape((8, neurons), F32),
            shape((GROUP, GROUP), BF),
            shape((GROUP, GROUP), BF),
            shape((2 * rim, neurons), BF),
            shape((rim, frames), BF),
            pltpu.VMEM((extended, neurons), BF),
        ],
        [WHOLE] * 4,
        [WHOLE] * 7,
        1.2,
    )(count, recording, footprints, traces)
    new_tr, rounded, far, near = call(
        sweep_kernel,
        [
            pltpu.VMEM((frames, neurons), F32),
            pltpu.VMEM((frames, neurons), BF),
            pltpu.VMEM((rim, frames), BF),
            pltpu.VMEM((rim, frames), BF),
        ],
        [WHOLE] * 8,
        [WHOLE] * 4,
        0.5,
    )(plan, scale, cross_high, cross_low, rims, flat, far, near)
    if split:
        return halved(voxels, rim, masked, recording, flat, outgoing[0], new_tr, rounded, far, near)
    return new_tr, spread(voxels, rim, masked, recording, rounded)


def solution(mesh):
    placed = (P("tm", "slab"), P(None, "slab"), P("tm", "slab"), P())
    return jax.shard_map(
        on_device,
        mesh=mesh,
        in_specs=placed,
        out_specs=(P("tm", "slab"), P("tm", "slab")),
        check_vma=False,
    )
```

profile of v0, /device:TPU:24, one launch (start us, length us, event | category | flops | bytes accessed | tf_op | source)
XLA Modules:
  0.0 22.6 jit_solution(16088924816047666676)
XLA Ops:
  0.6 0.0 copy-start
  0.6 0.0 copy-start.2
  0.7 0.0 copy-start.1
  0.7 1.6 %shard_map.59 = (bf16[256,128]{1,0:T(8,128)(2,1)S(1)}, bf16[256,128]{1,0:T(8,128)(2,1)S(1)}, s32[8,256]{1,0:T(8,128)S(1)}, bf16[1920,128]{1,0:T(8,128)(2,1)S(1)}) custom-call(s32[16]{0:T(128)} %live.1, bf16[256,2048]{1,0:T(8,128)(2,1)} %movie.5, bf16[2176,256]{1,0:T(8,128)(2,1)} %foot.3, f32[256,256]{1,0:T(8,128)} %start.3), custom_call_target="tpu_custom_call" | custom-call | bytes 5535000 | tf_op jit(solution)/shard_map/pallas_call | solution.py:356
  2.3 1.6 %collective-permute-start.2 = (bf16[1920,128]{1,0:T(8,128)(2,1)S(1)}, bf16[1920,128]{1,0:T(8,128)(2,1)S(1)}, u32[]{:S(2)}, u32[]{:S(2)}) collective-permute-start(bf16[1920,128]{1,0:T(8,128)(2,1)S(1)} %get-tuple-element.38), channel_id=1, source_target_pairs={{0,1},{1,0},{2,3},{3,2},{4,5},{5,4},{6,7},{7,6},{8,9},{9,8},{10,11... | collective-permute-start | bytes 1474568 | tf_op jit(solution)/shard_map/ppermute | solution.py:274
  3.8 2.5 %collective-permute-start = (bf16[256,128]{1,0:T(8,128)(2,1)S(1)}, bf16[256,128]{1,0:T(8,128)(2,1)S(1)}, u32[]{:S(2)}, u32[]{:S(2)}) collective-permute-start(bf16[256,128]{1,0:T(8,128)(2,1)S(1)} %get-tuple-element.33), channel_id=1, source_target_pairs={{2,4},{6,8},{10,12},{14,16},{18,20},{22,24},{26,28},{4,2},{8,6},{1... | collective-permute-start | bytes 196616 | tf_op jit(solution)/shard_map/ppermute | solution.py:266
  6.3 1.1 %collective-permute-start.1 = (bf16[256,128]{1,0:T(8,128)(2,1)S(1)}, bf16[256,128]{1,0:T(8,128)(2,1)S(1)}, u32[]{:S(2)}, u32[]{:S(2)}) collective-permute-start(bf16[256,128]{1,0:T(8,128)(2,1)S(1)} %get-tuple-element.34), channel_id=1, source_target_pairs={{0,2},{4,6},{8,10},{12,14},{16,18},{20,22},{24,26},{28,30},{2,0},{... | collective-permute-start | bytes 196616 | tf_op jit(solution)/shard_map/ppermute | solution.py:266
  7.4 0.0 copy-done
  7.4 0.0 copy-done.2
  7.4 0.0 copy-done.1
  7.4 1.2 %shard_map.60 = (f32[256,256]{1,0:T(8,128)S(1)}, f32[8,256]{1,0:T(8,128)S(1)}, bf16[128,128]{1,0:T(8,128)(2,1)S(1)}, bf16[128,128]{1,0:T(8,128)(2,1)S(1)}, bf16[...) custom-call(s32[8,256]{1,0:T(8,128)S(1)} %get-tuple-element.25.count, ...), custom_call_target="tpu_custom_call" | custom-call | bytes 4428000 | tf_op jit(solution)/shard_map/pallas_call | solution.py:379
  8.7 1.6 %collective-permute-done.far = bf16[256,128]{1,0:T(8,128)(2,1)S(1)} collective-permute-done((bf16[256,128]{1,0:T(8,128)(2,1)S(1)}, bf16[256,128]{1,0:T(8,128)(2,1)S(1)}, u32[]{:S(2)}, u32[]{:S(2)}) %collective-permute-start) | collective-permute-done | bytes 65568 | tf_op jit(solution)/shard_map/ppermute | solution.py:266
  10.3 0.0 collective-permute-done.1.near
  10.3 0.6 %shard_map.61 = (f32[256,256]{1,0:T(8,128)S(1)}, bf16[256,256]{1,0:T(8,128)(2,1)S(1)}, bf16[128,256]{1,0:T(8,128)(2,1)S(1)}, bf16[128,256]{1,0:T(8,128)(2,1)S(1)}) custom-call(f32[256,256]{1,0:T(8,128)S(1)} %get-tuple-element.27.plan, f32[8,256]{1,0:T(8,128)S(1)} %get-tuple-element.28.scale, bf16[128,128]{1,0:T(8,128)(2,1)S(1)} %get-tuple-element.29.cross_high, ...), custom_call_target="tpu_custom_call" | custom-call | bytes 1845000 | tf_op jit(solution)/shard_map/pallas_call | solution.py:394
  10.9 2.5 %collective-permute-start.4 = (bf16[128,256]{1,0:T(8,128)(2,1)S(1)}, bf16[128,256]{1,0:T(8,128)(2,1)S(1)}, u32[]{:S(2)}, u32[]{:S(2)}) collective-permute-start(bf16[128,256]{1,0:T(8,128)(2,1)S(1)} %get-tuple-element.43), channel_id=1, source_target_pairs={{2,4},{6,8},{10,12},{14,16},{18,20},{22,24},{26,28},{4,2},{8,6},{1... | collective-permute-start | bytes 196616 | tf_op jit(solution)/shard_map/ppermute | solution.py:266
  13.5 0.6 %collective-permute-start.3 = (bf16[256,256]{1,0:T(8,128)(2,1)S(1)}, bf16[256,256]{1,0:T(8,128)(2,1)S(1)}, u32[]{:S(2)}, u32[]{:S(2)}) collective-permute-start(bf16[256,256]{1,0:T(8,128)(2,1)S(1)} %get-tuple-element.35.fit), channel_id=1, source_target_pairs={{0,1},{1,0},{2,3},{3,2},{4,5},{5,4},{6,7},{7,6},{8,9},{9,8},{10,11... | collective-permute-start | bytes 393224 | tf_op jit(solution)/shard_map/ppermute | solution.py:277
  14.1 0.0 collective-permute-start.5
  14.1 0.6 %shard_map.62 = (f32[1024,256]{1,0:T(8,128)S(1)}, f32[256,256]{1,0:T(8,128)S(1)}, f32[256,256]{1,0:T(8,128)S(1)}) custom-call(bf16[256,2048]{1,0:T(8,128)(2,1)S(1)} %copy-done, bf16[2176,256]{1,0:T(8,128)(2,1)S(1)} %get-tuple-element.26.foot, bf16[256,256]{1,0:T(8,128)(2,1)S(1)} %get-tuple-element.35.fit, bf16[128,256]{1,0:T(8,128)(2,1)S(1)} %get-tuple-element.32.flat), custom_call_target="tpu_custom_call" | custom-call | bytes 2214000 | tf_op jit(solution)/shard_map/pallas_call | solution.py:278
  14.7 2.7 %collective-permute-done.4.far = bf16[128,256]{1,0:T(8,128)(2,1)S(1)} collective-permute-done((bf16[128,256]{1,0:T(8,128)(2,1)S(1)}, bf16[128,256]{1,0:T(8,128)(2,1)S(1)}, u32[]{:S(2)}, u32[]{:S(2)}) %collective-permute-start.4) | collective-permute-done | bytes 65568 | tf_op jit(solution)/shard_map/ppermute | solution.py:266
  17.4 0.0 collective-permute-done.5.near
  17.4 0.2 shard_map.64
  17.6 0.6 %collective-permute-start.6 = (bf16[128,256]{1,0:T(8,128)(2,1)S(1)}, bf16[128,256]{1,0:T(8,128)(2,1)S(1)}, u32[]{:S(2)}, u32[]{:S(2)}) collective-permute-start(bf16[128,256]{1,0:T(8,128)(2,1)S(1)} %get-tuple-element.46), channel_id=1, source_target_pairs={{0,1},{1,0},{2,3},{3,2},{4,5},{5,4},{6,7},{7,6},{8,9},{9,8},{10,11... | collective-permute-start | bytes 196616 | tf_op jit(solution)/shard_map/ppermute | solution.py:296
  18.2 1.1 %collective-permute-done.3.fit = bf16[256,256]{1,0:T(8,128)(2,1)S(1)} collective-permute-done((bf16[256,256]{1,0:T(8,128)(2,1)S(1)}, bf16[256,256]{1,0:T(8,128)(2,1)S(1)}, u32[]{:S(2)}, u32[]{:S(2)}) %collective-permute-start.3) | collective-permute-done | bytes 131104 | tf_op jit(solution)/shard_map/ppermute | solution.py:277
  19.4 0.0 collective-permute-done.2.movie
  19.4 1.5 %shard_map.63 = (bf16[1088,256]{1,0:T(8,128)(2,1)}, f32[256,256]{1,0:T(8,128)}, f32[8,256]{1,0:T(8,128)S(1)}) custom-call(bf16[2176,256]{1,0:T(8,128)(2,1)S(1)} %get-tuple-element.26.foot, f32[1024,256]{1,0:T(8,128)S(1)} %get-tuple-element.36.total, f32[256,256]{1,0:T(8,128)S(1)} %get-tuple-element.37.quad, ...), custom_call_target="tpu_custom_call" | custom-call | bytes 7380000 | tf_op jit(solution)/shard_map/pallas_call | solution.py:297
  20.9 1.0 %collective-permute-done.6.came = bf16[128,256]{1,0:T(8,128)(2,1)S(1)} collective-permute-done((bf16[128,256]{1,0:T(8,128)(2,1)S(1)}, bf16[128,256]{1,0:T(8,128)(2,1)S(1)}, u32[]{:S(2)}, u32[]{:S(2)}) %collective-permute-start.6) | collective-permute-done | bytes 65568 | tf_op jit(solution)/shard_map/ppermute | solution.py:296
  22.0 0.7 %shard_map.65 = bf16[1088,256]{1,0:T(8,128)(2,1)} custom-call(bf16[1088,256]{1,0:T(8,128)(2,1)} %get-tuple-element.41.sofar, bf16[2176,256]{1,0:T(8,128)(2,1)S(1)} %get-tuple-element.26.foot, f32[128,256]{1,0:T(8,128)S(1)} %get-tuple-element.45.lead, bf16[128,256]{1,0:T(8,128)(2,1)S(1)} %collective-permute-done.6.came, ...), custom_call_target="tpu_custom_call", output_to_operand_aliasing={{}: (0, {})} | custom-call | bytes 2952000 | tf_op jit(solution)/shard_map/pallas_call | solution.py:305
Async XLA Ops:
  0.6 6.8 %copy-start = (bf16[256,2048]{1,0:T(8,128)(2,1)S(1)}, bf16[256,2048]{1,0:T(8,128)(2,1)}, u32[]{:S(2)}) copy-start(bf16[256,2048]{1,0:T(8,128)(2,1)} %movie.5) | copy-start | bytes 3145732
  0.6 6.8 %copy-start.2 = (f32[256,256]{1,0:T(8,128)S(1)}, f32[256,256]{1,0:T(8,128)}, u32[]{:S(2)}) copy-start(f32[256,256]{1,0:T(8,128)} %start.3) | copy-start | bytes 786436
  0.7 6.8 %copy-start.1 = (bf16[2176,256]{1,0:T(8,128)(2,1)S(1)}, bf16[2176,256]{1,0:T(8,128)(2,1)}, u32[]{:S(2)}) copy-start(bf16[2176,256]{1,0:T(8,128)(2,1)} %foot.3) | copy-start | bytes 3342340
  2.3 17.1 %collective-permute-start.2 = (bf16[1920,128]{1,0:T(8,128)(2,1)S(1)}, bf16[1920,128]{1,0:T(8,128)(2,1)S(1)}, u32[]{:S(2)}, u32[]{:S(2)}) collective-permute-start(bf16[1920,128]{1,0:T(8,128)(2,1)S(1)} %get-tuple-element.38), channel_id=1, source_target_pairs={{0,1},{1,0},{2,3},{3,2},{4,5},{5,4},{6,7},{7,6},{8,9},{9,8},{10,11... | collective-permute-start | bytes 1474568 | tf_op jit(solution)/shard_map/ppermute | solution.py:274
  3.8 6.5 %collective-permute-start = (bf16[256,128]{1,0:T(8,128)(2,1)S(1)}, bf16[256,128]{1,0:T(8,128)(2,1)S(1)}, u32[]{:S(2)}, u32[]{:S(2)}) collective-permute-start(bf16[256,128]{1,0:T(8,128)(2,1)S(1)} %get-tuple-element.33), channel_id=1, source_target_pairs={{2,4},{6,8},{10,12},{14,16},{18,20},{22,24},{26,28},{4,2},{8,6},{1... | collective-permute-start | bytes 196616 | tf_op jit(solution)/shard_map/ppermute | solution.py:266
  6.3 4.0 %collective-permute-start.1 = (bf16[256,128]{1,0:T(8,128)(2,1)S(1)}, bf16[256,128]{1,0:T(8,128)(2,1)S(1)}, u32[]{:S(2)}, u32[]{:S(2)}) collective-permute-start(bf16[256,128]{1,0:T(8,128)(2,1)S(1)} %get-tuple-element.34), channel_id=1, source_target_pairs={{0,2},{4,6},{8,10},{12,14},{16,18},{20,22},{24,26},{28,30},{2,0},{... | collective-permute-start | bytes 196616 | tf_op jit(solution)/shard_map/ppermute | solution.py:266
  10.9 6.5 %collective-permute-start.4 = (bf16[128,256]{1,0:T(8,128)(2,1)S(1)}, bf16[128,256]{1,0:T(8,128)(2,1)S(1)}, u32[]{:S(2)}, u32[]{:S(2)}) collective-permute-start(bf16[128,256]{1,0:T(8,128)(2,1)S(1)} %get-tuple-element.43), channel_id=1, source_target_pairs={{2,4},{6,8},{10,12},{14,16},{18,20},{22,24},{26,28},{4,2},{8,6},{1... | collective-permute-start | bytes 196616 | tf_op jit(solution)/shard_map/ppermute | solution.py:266
  13.5 5.9 %collective-permute-start.3 = (bf16[256,256]{1,0:T(8,128)(2,1)S(1)}, bf16[256,256]{1,0:T(8,128)(2,1)S(1)}, u32[]{:S(2)}, u32[]{:S(2)}) collective-permute-start(bf16[256,256]{1,0:T(8,128)(2,1)S(1)} %get-tuple-element.35.fit), channel_id=1, source_target_pairs={{0,1},{1,0},{2,3},{3,2},{4,5},{5,4},{6,7},{7,6},{8,9},{9,8},{10,11... | collective-permute-start | bytes 393224 | tf_op jit(solution)/shard_map/ppermute | solution.py:277
  14.1 3.3 %collective-permute-start.5 = (bf16[128,256]{1,0:T(8,128)(2,1)S(1)}, bf16[128,256]{1,0:T(8,128)(2,1)S(1)}, u32[]{:S(2)}, u32[]{:S(2)}) collective-permute-start(bf16[128,256]{1,0:T(8,128)(2,1)S(1)} %get-tuple-element.44), channel_id=1, source_target_pairs={{0,2},{4,6},{8,10},{12,14},{16,18},{20,22},{24,26},{28,30},{2,0},{... | collective-permute-start | bytes 196616 | tf_op jit(solution)/shard_map/ppermute | solution.py:266
  17.6 4.3 %collective-permute-start.6 = (bf16[128,256]{1,0:T(8,128)(2,1)S(1)}, bf16[128,256]{1,0:T(8,128)(2,1)S(1)}, u32[]{:S(2)}, u32[]{:S(2)}) collective-permute-start(bf16[128,256]{1,0:T(8,128)(2,1)S(1)} %get-tuple-element.46), channel_id=1, source_target_pairs={{0,1},{1,0},{2,3},{3,2},{4,5},{5,4},{6,7},{7,6},{8,9},{9,8},{10,11... | collective-permute-start | bytes 196616 | tf_op jit(solution)/shard_map/ppermute | solution.py:296
where the time goes:
time: 22.8 us; the launch traced here: 22.6 us
  starting transfers between devices  8.9 us (39%)
  waiting for transfers between devices  6.54 us (29%)
  Pallas kernels  6.47 us (28%)
  between operations  0.71 us (3%)
    ppermute x4, starting transfers between devices, swapped(): return lax.ppermute(block, 'slab', route + [(j, i) for i, j in route])  6.14 us
    ppermute x4, waiting for transfers between devices, swapped(): return lax.ppermute(block, 'slab', route + [(j, i) for i, j in route])  4.35 us
    pallas_call x1, Pallas kernels, on_device(): call(functools.partial(rim_kernel, voxels), [pltpu.VMEM((frames, rim), BF...  1.6 us
    ppermute x1, starting transfers between devices, halved(): movie = lax.ppermute(outgoing, 'tm', across)  1.56 us
    pallas_call x1, Pallas kernels, halved(): call(functools.partial(main_kernel, voxels, rim), [pltpu.HBM((share, neur...  1.53 us
    pallas_call x1, Pallas kernels, on_device(): call(functools.partial(drive_kernel, voxels), [shape((frames, neurons), F...  1.22 us
    ppermute x1, waiting for transfers between devices, halved(): other = lax.ppermute(rounded, 'tm', across)  1.15 us
    ppermute x1, waiting for transfers between devices, halved(): came = lax.ppermute(sent, 'tm', across)  1.04 us
  transfers between devices with their start and end apart: 7, of which 4 were waited for; matrix products, arithmetic and copies ran while one was open for 0% of the time, Pallas kernels for 19%

commit v1 on v0

--- a/solution.py
+++ b/solution.py
@@ -108,20 +108,20 @@
 
 
 def rim_kernel(voxels, live, movie, foot, start, far, near, count, *rest):
-    numbers, head, tail, traces, edge, middle, sems = rest[-7:]
-    rim = head.shape[0]
+    numbers, rims, traces, edge, middle, sems = rest[-6:]
+    rim = edge.shape[1]
     frames = edge.shape[0]
     there = 1 - lax.axis_index("tm")
     small = [
         copied(live, numbers, sems.at[0]),
         copied(start, traces, sems.at[1]),
-        copied(foot.at[pl.ds(0, rim)], head, sems.at[2]),
-        copied(foot.at[pl.ds(voxels, rim)], tail, sems.at[3]),
+        copied(foot.at[pl.ds(0, rim)], rims.at[pl.ds(0, rim)], sems.at[2]),
+        copied(foot.at[pl.ds(voxels, rim)], rims.at[pl.ds(rim, rim)], sems.at[3]),
         copied(movie.at[:, pl.ds(0, rim)], edge, sems.at[4]),
         copied(movie.at[:, pl.ds(voxels // 2, rim)], middle, sems.at[5]),
     ]
     large = []
-    if len(rest) > 7:
+    if len(rest) > 6:
         first = first_column(there, voxels, rim)
         for i in range(voxels // 2 // rim - 1):
             column = movie.at[:, pl.ds(pl.multiple_of(first + i * rim, 128), rim)]
@@ -130,11 +130,9 @@
         copy.wait()
     alive = numbers[lax.axis_index("slab")]
     count[...] = jnp.full(count.shape, alive, jnp.int32)
-    high, low = halves(living(alive, traces[...]))
-    ends = jnp.where(at_end("slab"), jnp.zeros_like(tail[...]), tail[...])
-    forward = mm_t(high, ends) + mm_t(low, ends)
-    backward = edge[...].astype(F32) - (mm_t(high, head[...]) + mm_t(low, head[...]))
-    one, two = for_near_and_far(forward, backward)
+    seen = mm_t(living(alive, traces[...]).astype(BF), rims[...])
+    backward = edge[...].astype(F32) - seen[:, :rim]
+    one, two = for_near_and_far(seen[:, rim:], backward)
     near[...] = one.astype(BF)
     far[...] = two.astype(BF)
     if large:
@@ -182,9 +180,8 @@
     second = jnp.maximum(stepped[:, GROUP:] - coupled * scale[0:1, GROUP:], 0.0)
     whole = jnp.concatenate([high, second.astype(BF)], axis=1)
     rounded[...] = whole
-    forward = mm_t(edges[rim:], whole)
-    backward = flat[...].astype(F32) + mm_t(edges[:rim], whole)
-    one, two = for_near_and_far(forward, backward)
+    seen = mm_t(edges, whole)
+    one, two = for_near_and_far(seen[rim:], flat[...].astype(F32) + seen[:rim])
     near_next[...] = one.astype(BF)
     far_next[...] = two.astype(BF)
     traces[:, :GROUP] = first
@@ -366,8 +363,7 @@
         1.5,
         scratch_shapes=[
             pltpu.SMEM(live_count.shape, jnp.int32),
-            pltpu.VMEM((rim, neurons), BF),
-            pltpu.VMEM((rim, neurons), BF),
+            pltpu.VMEM((2 * rim, neurons), BF),
             pltpu.VMEM((frames, neurons), F32),
             pltpu.VMEM((frames, rim), BF),
             pltpu.VMEM((frames, rim), BF),

time: 22.8 us -> 22.7 us (level)
  no operation moved by 1% of the time
where the time goes in v1:
time: 22.7 us; the launch traced here: 22.5 us
  starting transfers between devices  8.9 us (39%)
  waiting for transfers between devices  6.55 us (29%)
  Pallas kernels  6.36 us (28%)
  between operations  0.72 us (3%)
    ppermute x4, starting transfers between devices, swapped(): return lax.ppermute(block, 'slab', route + [(j, i) for i, j in route])  6.14 us
    ppermute x4, waiting for transfers between devices, swapped(): return lax.ppermute(block, 'slab', route + [(j, i) for i, j in route])  4.35 us
    ppermute x1, starting transfers between devices, halved(): movie = lax.ppermute(outgoing, 'tm', across)  1.56 us
    pallas_call x1, Pallas kernels, halved(): call(functools.partial(main_kernel, voxels, rim), [pltpu.HBM((share, neur...  1.53 us
    pallas_call x1, Pallas kernels, on_device(): call(functools.partial(rim_kernel, voxels), [pltpu.VMEM((frames, rim), BF...  1.52 us
    pallas_call x1, Pallas kernels, on_device(): call(functools.partial(drive_kernel, voxels), [shape((frames, neurons), F...  1.23 us
    ppermute x1, waiting for transfers between devices, halved(): other = lax.ppermute(rounded, 'tm', across)  1.14 us
    ppermute x1, waiting for transfers between devices, halved(): came = lax.ppermute(sent, 'tm', across)  1.06 us
  transfers between devices with their start and end apart: 7, of which 4 were waited for; matrix products, arithmetic and copies ran while one was open for 0% of the time, Pallas kernels for 19%

profile of v1, /device:TPU:24, one launch (start us, length us, event | category | flops | bytes accessed | tf_op | source)
XLA Modules:
  0.0 22.5 jit_solution(10281840986731058955)
XLA Ops:
  0.6 0.0 copy-start
  0.6 0.0 copy-start.2
  0.7 0.0 copy-start.1
  0.7 1.5 %shard_map.59 = (bf16[256,128]{1,0:T(8,128)(2,1)S(1)}, bf16[256,128]{1,0:T(8,128)(2,1)S(1)}, s32[8,256]{1,0:T(8,128)S(1)}, bf16[1920,128]{1,0:T(8,128)(2,1)S(1)}) custom-call(s32[16]{0:T(128)} %live.1, bf16[256,2048]{1,0:T(8,128)(2,1)} %movie.5, bf16[2176,256]{1,0:T(8,128)(2,1)} %foot.3, f32[256,256]{1,0:T(8,128)} %start.3), custom_call_target="tpu_custom_call" | custom-call | bytes 5535000 | tf_op jit(solution)/shard_map/pallas_call | solution.py:353
  2.2 1.6 %collective-permute-start.2 = (bf16[1920,128]{1,0:T(8,128)(2,1)S(1)}, bf16[1920,128]{1,0:T(8,128)(2,1)S(1)}, u32[]{:S(2)}, u32[]{:S(2)}) collective-permute-start(bf16[1920,128]{1,0:T(8,128)(2,1)S(1)} %get-tuple-element.38), channel_id=1, source_target_pairs={{0,1},{1,0},{2,3},{3,2},{4,5},{5,4},{6,7},{7,6},{8,9},{9,8},{10,11... | collective-permute-start | bytes 1474568 | tf_op jit(solution)/shard_map/ppermute | solution.py:271
  3.7 2.5 %collective-permute-start = (bf16[256,128]{1,0:T(8,128)(2,1)S(1)}, bf16[256,128]{1,0:T(8,128)(2,1)S(1)}, u32[]{:S(2)}, u32[]{:S(2)}) collective-permute-start(bf16[256,128]{1,0:T(8,128)(2,1)S(1)} %get-tuple-element.33), channel_id=1, source_target_pairs={{2,4},{6,8},{10,12},{14,16},{18,20},{22,24},{26,28},{4,2},{8,6},{1... | collective-permute-start | bytes 196616 | tf_op jit(solution)/shard_map/ppermute | solution.py:263
  6.2 1.1 %collective-permute-start.1 = (bf16[256,128]{1,0:T(8,128)(2,1)S(1)}, bf16[256,128]{1,0:T(8,128)(2,1)S(1)}, u32[]{:S(2)}, u32[]{:S(2)}) collective-permute-start(bf16[256,128]{1,0:T(8,128)(2,1)S(1)} %get-tuple-element.34), channel_id=1, source_target_pairs={{0,2},{4,6},{8,10},{12,14},{16,18},{20,22},{24,26},{28,30},{2,0},{... | collective-permute-start | bytes 196616 | tf_op jit(solution)/shard_map/ppermute | solution.py:263
  7.3 0.0 copy-done
  7.3 0.0 copy-done.2
  7.4 0.0 copy-done.1
  7.4 1.2 %shard_map.60 = (f32[256,256]{1,0:T(8,128)S(1)}, f32[8,256]{1,0:T(8,128)S(1)}, bf16[128,128]{1,0:T(8,128)(2,1)S(1)}, bf16[128,128]{1,0:T(8,128)(2,1)S(1)}, bf16[...) custom-call(s32[8,256]{1,0:T(8,128)S(1)} %get-tuple-element.25.count, ...), custom_call_target="tpu_custom_call" | custom-call | bytes 4428000 | tf_op jit(solution)/shard_map/pallas_call | solution.py:375
  8.6 1.6 %collective-permute-done.far = bf16[256,128]{1,0:T(8,128)(2,1)S(1)} collective-permute-done((bf16[256,128]{1,0:T(8,128)(2,1)S(1)}, bf16[256,128]{1,0:T(8,128)(2,1)S(1)}, u32[]{:S(2)}, u32[]{:S(2)}) %collective-permute-start) | collective-permute-done | bytes 65568 | tf_op jit(solution)/shard_map/ppermute | solution.py:263
  10.2 0.0 collective-permute-done.1.near
  10.2 0.6 %shard_map.61 = (f32[256,256]{1,0:T(8,128)S(1)}, bf16[256,256]{1,0:T(8,128)(2,1)S(1)}, bf16[128,256]{1,0:T(8,128)(2,1)S(1)}, bf16[128,256]{1,0:T(8,128)(2,1)S(1)}) custom-call(f32[256,256]{1,0:T(8,128)S(1)} %get-tuple-element.27.plan, f32[8,256]{1,0:T(8,128)S(1)} %get-tuple-element.28.scale, bf16[128,128]{1,0:T(8,128)(2,1)S(1)} %get-tuple-element.29.cross_high, ...), custom_call_target="tpu_custom_call" | custom-call | bytes 1845000 | tf_op jit(solution)/shard_map/pallas_call | solution.py:390
  10.8 2.5 %collective-permute-start.4 = (bf16[128,256]{1,0:T(8,128)(2,1)S(1)}, bf16[128,256]{1,0:T(8,128)(2,1)S(1)}, u32[]{:S(2)}, u32[]{:S(2)}) collective-permute-start(bf16[128,256]{1,0:T(8,128)(2,1)S(1)} %get-tuple-element.43), channel_id=1, source_target_pairs={{2,4},{6,8},{10,12},{14,16},{18,20},{22,24},{26,28},{4,2},{8,6},{1... | collective-permute-start | bytes 196616 | tf_op jit(solution)/shard_map/ppermute | solution.py:263
  13.4 0.6 %collective-permute-start.3 = (bf16[256,256]{1,0:T(8,128)(2,1)S(1)}, bf16[256,256]{1,0:T(8,128)(2,1)S(1)}, u32[]{:S(2)}, u32[]{:S(2)}) collective-permute-start(bf16[256,256]{1,0:T(8,128)(2,1)S(1)} %get-tuple-element.35.fit), channel_id=1, source_target_pairs={{0,1},{1,0},{2,3},{3,2},{4,5},{5,4},{6,7},{7,6},{8,9},{9,8},{10,11... | collective-permute-start | bytes 393224 | tf_op jit(solution)/shard_map/ppermute | solution.py:274
  14.0 0.0 collective-permute-start.5
  14.0 0.6 %shard_map.62 = (f32[1024,256]{1,0:T(8,128)S(1)}, f32[256,256]{1,0:T(8,128)S(1)}, f32[256,256]{1,0:T(8,128)S(1)}) custom-call(bf16[256,2048]{1,0:T(8,128)(2,1)S(1)} %copy-done, bf16[2176,256]{1,0:T(8,128)(2,1)S(1)} %get-tuple-element.26.foot, bf16[256,256]{1,0:T(8,128)(2,1)S(1)} %get-tuple-element.35.fit, bf16[128,256]{1,0:T(8,128)(2,1)S(1)} %get-tuple-element.32.flat), custom_call_target="tpu_custom_call" | custom-call | bytes 2214000 | tf_op jit(solution)/shard_map/pallas_call | solution.py:275
  14.6 2.7 %collective-permute-done.4.far = bf16[128,256]{1,0:T(8,128)(2,1)S(1)} collective-permute-done((bf16[128,256]{1,0:T(8,128)(2,1)S(1)}, bf16[128,256]{1,0:T(8,128)(2,1)S(1)}, u32[]{:S(2)}, u32[]{:S(2)}) %collective-permute-start.4) | collective-permute-done | bytes 65568 | tf_op jit(solution)/shard_map/ppermute | solution.py:263
  17.3 0.0 collective-permute-done.5.near
  17.3 0.2 shard_map.64
  17.5 0.6 %collective-permute-start.6 = (bf16[128,256]{1,0:T(8,128)(2,1)S(1)}, bf16[128,256]{1,0:T(8,128)(2,1)S(1)}, u32[]{:S(2)}, u32[]{:S(2)}) collective-permute-start(bf16[128,256]{1,0:T(8,128)(2,1)S(1)} %get-tuple-element.46), channel_id=1, source_target_pairs={{0,1},{1,0},{2,3},{3,2},{4,5},{5,4},{6,7},{7,6},{8,9},{9,8},{10,11... | collective-permute-start | bytes 196616 | tf_op jit(solution)/shard_map/ppermute | solution.py:293
  18.1 1.1 %collective-permute-done.3.fit = bf16[256,256]{1,0:T(8,128)(2,1)S(1)} collective-permute-done((bf16[256,256]{1,0:T(8,128)(2,1)S(1)}, bf16[256,256]{1,0:T(8,128)(2,1)S(1)}, u32[]{:S(2)}, u32[]{:S(2)}) %collective-permute-start.3) | collective-permute-done | bytes 131104 | tf_op jit(solution)/shard_map/ppermute | solution.py:274
  19.3 0.0 collective-permute-done.2.movie
  19.3 1.5 %shard_map.63 = (bf16[1088,256]{1,0:T(8,128)(2,1)}, f32[256,256]{1,0:T(8,128)}, f32[8,256]{1,0:T(8,128)S(1)}) custom-call(bf16[2176,256]{1,0:T(8,128)(2,1)S(1)} %get-tuple-element.26.foot, f32[1024,256]{1,0:T(8,128)S(1)} %get-tuple-element.36.total, f32[256,256]{1,0:T(8,128)S(1)} %get-tuple-element.37.quad, ...), custom_call_target="tpu_custom_call" | custom-call | bytes 7380000 | tf_op jit(solution)/shard_map/pallas_call | solution.py:294
  20.8 1.1 %collective-permute-done.6.came = bf16[128,256]{1,0:T(8,128)(2,1)S(1)} collective-permute-done((bf16[128,256]{1,0:T(8,128)(2,1)S(1)}, bf16[128,256]{1,0:T(8,128)(2,1)S(1)}, u32[]{:S(2)}, u32[]{:S(2)}) %collective-permute-start.6) | collective-permute-done | bytes 65568 | tf_op jit(solution)/shard_map/ppermute | solution.py:293
  21.9 0.7 %shard_map.65 = bf16[1088,256]{1,0:T(8,128)(2,1)} custom-call(bf16[1088,256]{1,0:T(8,128)(2,1)} %get-tuple-element.41.sofar, bf16[2176,256]{1,0:T(8,128)(2,1)S(1)} %get-tuple-element.26.foot, f32[128,256]{1,0:T(8,128)S(1)} %get-tuple-element.45.lead, bf16[128,256]{1,0:T(8,128)(2,1)S(1)} %collective-permute-done.6.came, ...), custom_call_target="tpu_custom_call", output_to_operand_aliasing={{}: (0, {})} | custom-call | bytes 2952000 | tf_op jit(solution)/shard_map/pallas_call | solution.py:302
Async XLA Ops:
  0.6 6.7 %copy-start = (bf16[256,2048]{1,0:T(8,128)(2,1)S(1)}, bf16[256,2048]{1,0:T(8,128)(2,1)}, u32[]{:S(2)}) copy-start(bf16[256,2048]{1,0:T(8,128)(2,1)} %movie.5) | copy-start | bytes 3145732
  0.6 6.7 %copy-start.2 = (f32[256,256]{1,0:T(8,128)S(1)}, f32[256,256]{1,0:T(8,128)}, u32[]{:S(2)}) copy-start(f32[256,256]{1,0:T(8,128)} %start.3) | copy-start | bytes 786436
  0.7 6.7 %copy-start.1 = (bf16[2176,256]{1,0:T(8,128)(2,1)S(1)}, bf16[2176,256]{1,0:T(8,128)(2,1)}, u32[]{:S(2)}) copy-start(bf16[2176,256]{1,0:T(8,128)(2,1)} %foot.3) | copy-start | bytes 3342340
  2.2 17.1 %collective-permute-start.2 = (bf16[1920,128]{1,0:T(8,128)(2,1)S(1)}, bf16[1920,128]{1,0:T(8,128)(2,1)S(1)}, u32[]{:S(2)}, u32[]{:S(2)}) collective-permute-start(bf16[1920,128]{1,0:T(8,128)(2,1)S(1)} %get-tuple-element.38), channel_id=1, source_target_pairs={{0,1},{1,0},{2,3},{3,2},{4,5},{5,4},{6,7},{7,6},{8,9},{9,8},{10,11... | collective-permute-start | bytes 1474568 | tf_op jit(solution)/shard_map/ppermute | solution.py:271
  3.7 6.5 %collective-permute-start = (bf16[256,128]{1,0:T(8,128)(2,1)S(1)}, bf16[256,128]{1,0:T(8,128)(2,1)S(1)}, u32[]{:S(2)}, u32[]{:S(2)}) collective-permute-start(bf16[256,128]{1,0:T(8,128)(2,1)S(1)} %get-tuple-element.33), channel_id=1, source_target_pairs={{2,4},{6,8},{10,12},{14,16},{18,20},{22,24},{26,28},{4,2},{8,6},{1... | collective-permute-start | bytes 196616 | tf_op jit(solution)/shard_map/ppermute | solution.py:263
  6.2 4.0 %collective-permute-start.1 = (bf16[256,128]{1,0:T(8,128)(2,1)S(1)}, bf16[256,128]{1,0:T(8,128)(2,1)S(1)}, u32[]{:S(2)}, u32[]{:S(2)}) collective-permute-start(bf16[256,128]{1,0:T(8,128)(2,1)S(1)} %get-tuple-element.34), channel_id=1, source_target_pairs={{0,2},{4,6},{8,10},{12,14},{16,18},{20,22},{24,26},{28,30},{2,0},{... | collective-permute-start | bytes 196616 | tf_op jit(solution)/shard_map/ppermute | solution.py:263
  10.8 6.5 %collective-permute-start.4 = (bf16[128,256]{1,0:T(8,128)(2,1)S(1)}, bf16[128,256]{1,0:T(8,128)(2,1)S(1)}, u32[]{:S(2)}, u32[]{:S(2)}) collective-permute-start(bf16[128,256]{1,0:T(8,128)(2,1)S(1)} %get-tuple-element.43), channel_id=1, source_target_pairs={{2,4},{6,8},{10,12},{14,16},{18,20},{22,24},{26,28},{4,2},{8,6},{1... | collective-permute-start | bytes 196616 | tf_op jit(solution)/shard_map/ppermute | solution.py:263
  13.4 5.9 %collective-permute-start.3 = (bf16[256,256]{1,0:T(8,128)(2,1)S(1)}, bf16[256,256]{1,0:T(8,128)(2,1)S(1)}, u32[]{:S(2)}, u32[]{:S(2)}) collective-permute-start(bf16[256,256]{1,0:T(8,128)(2,1)S(1)} %get-tuple-element.35.fit), channel_id=1, source_target_pairs={{0,1},{1,0},{2,3},{3,2},{4,5},{5,4},{6,7},{7,6},{8,9},{9,8},{10,11... | collective-permute-start | bytes 393224 | tf_op jit(solution)/shard_map/ppermute | solution.py:274
  14.0 3.3 %collective-permute-start.5 = (bf16[128,256]{1,0:T(8,128)(2,1)S(1)}, bf16[128,256]{1,0:T(8,128)(2,1)S(1)}, u32[]{:S(2)}, u32[]{:S(2)}) collective-permute-start(bf16[128,256]{1,0:T(8,128)(2,1)S(1)} %get-tuple-element.44), channel_id=1, source_target_pairs={{0,2},{4,6},{8,10},{12,14},{16,18},{20,22},{24,26},{28,30},{2,0},{... | collective-permute-start | bytes 196616 | tf_op jit(solution)/shard_map/ppermute | solution.py:263
  17.5 4.3 %collective-permute-start.6 = (bf16[128,256]{1,0:T(8,128)(2,1)S(1)}, bf16[128,256]{1,0:T(8,128)(2,1)S(1)}, u32[]{:S(2)}, u32[]{:S(2)}) collective-permute-start(bf16[128,256]{1,0:T(8,128)(2,1)S(1)} %get-tuple-element.46), channel_id=1, source_target_pairs={{0,1},{1,0},{2,3},{3,2},{4,5},{5,4},{6,7},{7,6},{8,9},{9,8},{10,11... | collective-permute-start | bytes 196616 | tf_op jit(solution)/shard_map/ppermute | solution.py:293

commit v2 on v1

--- a/solution.py
+++ b/solution.py
@@ -176,7 +176,9 @@
     first = jnp.maximum(stepped[:, :GROUP], 0.0)
     high, low = halves(first)
     cross = cross_high[...]
-    coupled = mm(high, cross) + mm(high, cross_low[...]) + mm(low, cross)
+    coupled = mm(
+        jnp.concatenate([high, low, high], axis=1), jnp.concatenate([cross, cross, cross_low[...]], axis=0)
+    )
     second = jnp.maximum(stepped[:, GROUP:] - coupled * scale[0:1, GROUP:], 0.0)
     whole = jnp.concatenate([high, second.astype(BF)], axis=1)
     rounded[...] = whole
@@ -260,7 +262,7 @@
 
 def swapped(block, first):
     route = [(i, i + 1) for i in range(first, lax.axis_size("slab") - 1, 2)]
-    return lax.ppermute(block, "slab", route + [(j, i) for i, j in route])
+    return lax.ppermute(block, "slab", [(j, i) for i, j in route] + route)
 
 
 def halved(voxels, rim, foot, recording, flat, outgoing, new_tr, rounded, far, near):

time: 22.7 us -> 22.7 us (level)
  transfers between devices with their start and end apart: 7 -> 7, of which waited for: 4 -> 4; matrix products, arithmetic and copies ran while one was open for 0% -> 0% of each run, Pallas kernels for 19% -> 18%
where the time goes in v2:
time: 22.7 us; the launch traced here: 22.5 us
  starting transfers between devices  8.9 us (39%)
  waiting for transfers between devices  6.54 us (29%)
  Pallas kernels  6.33 us (28%)
  between operations  0.72 us (3%)
    ppermute x4, starting transfers between devices, swapped(): return lax.ppermute(block, 'slab', [(j, i) for i, j in route] + route)  6.14 us
    ppermute x4, waiting for transfers between devices, swapped(): return lax.ppermute(block, 'slab', [(j, i) for i, j in route] + route)  4.35 us
    ppermute x1, starting transfers between devices, halved(): movie = lax.ppermute(outgoing, 'tm', across)  1.56 us
    pallas_call x1, Pallas kernels, halved(): call(functools.partial(main_kernel, voxels, rim), [pltpu.HBM((share, neur...  1.53 us
    pallas_call x1, Pallas kernels, on_device(): call(functools.partial(rim_kernel, voxels), [pltpu.VMEM((frames, rim), BF...  1.52 us
    pallas_call x1, Pallas kernels, on_device(): call(functools.partial(drive_kernel, voxels), [shape((frames, neurons), F...  1.23 us
    ppermute x1, waiting for transfers between devices, halved(): other = lax.ppermute(rounded, 'tm', across)  1.14 us
    ppermute x1, waiting for transfers between devices, halved(): came = lax.ppermute(sent, 'tm', across)  1.05 us
  transfers between devices with their start and end apart: 7, of which 4 were waited for; matrix products, arithmetic and copies ran while one was open for 0% of the time, Pallas kernels for 18%

profile of v2, /device:TPU:24, one launch (start us, length us, event | category | flops | bytes accessed | tf_op | source)
XLA Modules:
  0.0 22.5 jit_solution(11040114047578464334)
XLA Ops:
  0.6 0.0 copy-start
  0.6 0.0 copy-start.2
  0.7 0.0 copy-start.1
  0.7 1.5 %shard_map.59 = (bf16[256,128]{1,0:T(8,128)(2,1)S(1)}, bf16[256,128]{1,0:T(8,128)(2,1)S(1)}, s32[8,256]{1,0:T(8,128)S(1)}, bf16[1920,128]{1,0:T(8,128)(2,1)S(1)}) custom-call(s32[16]{0:T(128)} %live.1, bf16[256,2048]{1,0:T(8,128)(2,1)} %movie.5, bf16[2176,256]{1,0:T(8,128)(2,1)} %foot.3, f32[256,256]{1,0:T(8,128)} %start.3), custom_call_target="tpu_custom_call" | custom-call | bytes 5535000 | tf_op jit(solution)/shard_map/pallas_call | solution.py:355
  2.2 1.6 %collective-permute-start.2 = (bf16[1920,128]{1,0:T(8,128)(2,1)S(1)}, bf16[1920,128]{1,0:T(8,128)(2,1)S(1)}, u32[]{:S(2)}, u32[]{:S(2)}) collective-permute-start(bf16[1920,128]{1,0:T(8,128)(2,1)S(1)} %get-tuple-element.38), channel_id=1, source_target_pairs={{0,1},{1,0},{2,3},{3,2},{4,5},{5,4},{6,7},{7,6},{8,9},{9,8},{10,11... | collective-permute-start | bytes 1474568 | tf_op jit(solution)/shard_map/ppermute | solution.py:273
  3.7 2.5 %collective-permute-start = (bf16[256,128]{1,0:T(8,128)(2,1)S(1)}, bf16[256,128]{1,0:T(8,128)(2,1)S(1)}, u32[]{:S(2)}, u32[]{:S(2)}) collective-permute-start(bf16[256,128]{1,0:T(8,128)(2,1)S(1)} %get-tuple-element.33), channel_id=1, source_target_pairs={{4,2},{8,6},{12,10},{16,14},{20,18},{24,22},{28,26},{2,4},{6,8},{1... | collective-permute-start | bytes 196616 | tf_op jit(solution)/shard_map/ppermute | solution.py:265
  6.2 1.1 %collective-permute-start.1 = (bf16[256,128]{1,0:T(8,128)(2,1)S(1)}, bf16[256,128]{1,0:T(8,128)(2,1)S(1)}, u32[]{:S(2)}, u32[]{:S(2)}) collective-permute-start(bf16[256,128]{1,0:T(8,128)(2,1)S(1)} %get-tuple-element.34), channel_id=1, source_target_pairs={{2,0},{6,4},{10,8},{14,12},{18,16},{22,20},{26,24},{30,28},{0,2},{... | collective-permute-start | bytes 196616 | tf_op jit(solution)/shard_map/ppermute | solution.py:265
  7.3 0.0 copy-done
  7.3 0.0 copy-done.2
  7.4 0.0 copy-done.1
  7.4 1.2 %shard_map.60 = (f32[256,256]{1,0:T(8,128)S(1)}, f32[8,256]{1,0:T(8,128)S(1)}, bf16[128,128]{1,0:T(8,128)(2,1)S(1)}, bf16[128,128]{1,0:T(8,128)(2,1)S(1)}, bf16[...) custom-call(s32[8,256]{1,0:T(8,128)S(1)} %get-tuple-element.25.count, ...), custom_call_target="tpu_custom_call" | custom-call | bytes 4428000 | tf_op jit(solution)/shard_map/pallas_call | solution.py:377
  8.6 1.6 %collective-permute-done.far = bf16[256,128]{1,0:T(8,128)(2,1)S(1)} collective-permute-done((bf16[256,128]{1,0:T(8,128)(2,1)S(1)}, bf16[256,128]{1,0:T(8,128)(2,1)S(1)}, u32[]{:S(2)}, u32[]{:S(2)}) %collective-permute-start) | collective-permute-done | bytes 65568 | tf_op jit(solution)/shard_map/ppermute | solution.py:265
  10.2 0.0 collective-permute-done.1.near
  10.2 0.6 %shard_map.61 = (f32[256,256]{1,0:T(8,128)S(1)}, bf16[256,256]{1,0:T(8,128)(2,1)S(1)}, bf16[128,256]{1,0:T(8,128)(2,1)S(1)}, bf16[128,256]{1,0:T(8,128)(2,1)S(1)}) custom-call(f32[256,256]{1,0:T(8,128)S(1)} %get-tuple-element.27.plan, f32[8,256]{1,0:T(8,128)S(1)} %get-tuple-element.28.scale, bf16[128,128]{1,0:T(8,128)(2,1)S(1)} %get-tuple-element.29.cross_high, ...), custom_call_target="tpu_custom_call" | custom-call | bytes 1845000 | tf_op jit(solution)/shard_map/pallas_call | solution.py:392
  10.8 2.5 %collective-permute-start.4 = (bf16[128,256]{1,0:T(8,128)(2,1)S(1)}, bf16[128,256]{1,0:T(8,128)(2,1)S(1)}, u32[]{:S(2)}, u32[]{:S(2)}) collective-permute-start(bf16[128,256]{1,0:T(8,128)(2,1)S(1)} %get-tuple-element.43), channel_id=1, source_target_pairs={{4,2},{8,6},{12,10},{16,14},{20,18},{24,22},{28,26},{2,4},{6,8},{1... | collective-permute-start | bytes 196616 | tf_op jit(solution)/shard_map/ppermute | solution.py:265
  13.4 0.6 %collective-permute-start.3 = (bf16[256,256]{1,0:T(8,128)(2,1)S(1)}, bf16[256,256]{1,0:T(8,128)(2,1)S(1)}, u32[]{:S(2)}, u32[]{:S(2)}) collective-permute-start(bf16[256,256]{1,0:T(8,128)(2,1)S(1)} %get-tuple-element.35.fit), channel_id=1, source_target_pairs={{0,1},{1,0},{2,3},{3,2},{4,5},{5,4},{6,7},{7,6},{8,9},{9,8},{10,11... | collective-permute-start | bytes 393224 | tf_op jit(solution)/shard_map/ppermute | solution.py:276
  14.0 0.0 collective-permute-start.5
  14.0 0.6 %shard_map.62 = (f32[1024,256]{1,0:T(8,128)S(1)}, f32[256,256]{1,0:T(8,128)S(1)}, f32[256,256]{1,0:T(8,128)S(1)}) custom-call(bf16[256,2048]{1,0:T(8,128)(2,1)S(1)} %copy-done, bf16[2176,256]{1,0:T(8,128)(2,1)S(1)} %get-tuple-element.26.foot, bf16[256,256]{1,0:T(8,128)(2,1)S(1)} %get-tuple-element.35.fit, bf16[128,256]{1,0:T(8,128)(2,1)S(1)} %get-tuple-element.32.flat), custom_call_target="tpu_custom_call" | custom-call | bytes 2214000 | tf_op jit(solution)/shard_map/pallas_call | solution.py:277
  14.6 2.7 %collective-permute-done.4.far = bf16[128,256]{1,0:T(8,128)(2,1)S(1)} collective-permute-done((bf16[128,256]{1,0:T(8,128)(2,1)S(1)}, bf16[128,256]{1,0:T(8,128)(2,1)S(1)}, u32[]{:S(2)}, u32[]{:S(2)}) %collective-permute-start.4) | collective-permute-done | bytes 65568 | tf_op jit(solution)/shard_map/ppermute | solution.py:265
  17.3 0.0 collective-permute-done.5.near
  17.3 0.2 shard_map.64
  17.5 0.6 %collective-permute-start.6 = (bf16[128,256]{1,0:T(8,128)(2,1)S(1)}, bf16[128,256]{1,0:T(8,128)(2,1)S(1)}, u32[]{:S(2)}, u32[]{:S(2)}) collective-permute-start(bf16[128,256]{1,0:T(8,128)(2,1)S(1)} %get-tuple-element.46), channel_id=1, source_target_pairs={{0,1},{1,0},{2,3},{3,2},{4,5},{5,4},{6,7},{7,6},{8,9},{9,8},{10,11... | collective-permute-start | bytes 196616 | tf_op jit(solution)/shard_map/ppermute | solution.py:295
  18.1 1.1 %collective-permute-done.3.fit = bf16[256,256]{1,0:T(8,128)(2,1)S(1)} collective-permute-done((bf16[256,256]{1,0:T(8,128)(2,1)S(1)}, bf16[256,256]{1,0:T(8,128)(2,1)S(1)}, u32[]{:S(2)}, u32[]{:S(2)}) %collective-permute-start.3) | collective-permute-done | bytes 131104 | tf_op jit(solution)/shard_map/ppermute | solution.py:276
  19.2 0.0 collective-permute-done.2.movie
  19.2 1.5 %shard_map.63 = (bf16[1088,256]{1,0:T(8,128)(2,1)}, f32[256,256]{1,0:T(8,128)}, f32[8,256]{1,0:T(8,128)S(1)}) custom-call(bf16[2176,256]{1,0:T(8,128)(2,1)S(1)} %get-tuple-element.26.foot, f32[1024,256]{1,0:T(8,128)S(1)} %get-tuple-element.36.total, f32[256,256]{1,0:T(8,128)S(1)} %get-tuple-element.37.quad, ...), custom_call_target="tpu_custom_call" | custom-call | bytes 7380000 | tf_op jit(solution)/shard_map/pallas_call | solution.py:296
  20.8 1.1 %collective-permute-done.6.came = bf16[128,256]{1,0:T(8,128)(2,1)S(1)} collective-permute-done((bf16[128,256]{1,0:T(8,128)(2,1)S(1)}, bf16[128,256]{1,0:T(8,128)(2,1)S(1)}, u32[]{:S(2)}, u32[]{:S(2)}) %collective-permute-start.6) | collective-permute-done | bytes 65568 | tf_op jit(solution)/shard_map/ppermute | solution.py:295
  21.8 0.7 %shard_map.65 = bf16[1088,256]{1,0:T(8,128)(2,1)} custom-call(bf16[1088,256]{1,0:T(8,128)(2,1)} %get-tuple-element.41.sofar, bf16[2176,256]{1,0:T(8,128)(2,1)S(1)} %get-tuple-element.26.foot, f32[128,256]{1,0:T(8,128)S(1)} %get-tuple-element.45.lead, bf16[128,256]{1,0:T(8,128)(2,1)S(1)} %collective-permute-done.6.came, ...), custom_call_target="tpu_custom_call", output_to_operand_aliasing={{}: (0, {})} | custom-call | bytes 2952000 | tf_op jit(solution)/shard_map/pallas_call | solution.py:304
Async XLA Ops:
  0.6 6.7 %copy-start = (bf16[256,2048]{1,0:T(8,128)(2,1)S(1)}, bf16[256,2048]{1,0:T(8,128)(2,1)}, u32[]{:S(2)}) copy-start(bf16[256,2048]{1,0:T(8,128)(2,1)} %movie.5) | copy-start | bytes 3145732
  0.6 6.7 %copy-start.2 = (f32[256,256]{1,0:T(8,128)S(1)}, f32[256,256]{1,0:T(8,128)}, u32[]{:S(2)}) copy-start(f32[256,256]{1,0:T(8,128)} %start.3) | copy-start | bytes 786436
  0.7 6.7 %copy-start.1 = (bf16[2176,256]{1,0:T(8,128)(2,1)S(1)}, bf16[2176,256]{1,0:T(8,128)(2,1)}, u32[]{:S(2)}) copy-start(bf16[2176,256]{1,0:T(8,128)(2,1)} %foot.3) | copy-start | bytes 3342340
  2.2 17.1 %collective-permute-start.2 = (bf16[1920,128]{1,0:T(8,128)(2,1)S(1)}, bf16[1920,128]{1,0:T(8,128)(2,1)S(1)}, u32[]{:S(2)}, u32[]{:S(2)}) collective-permute-start(bf16[1920,128]{1,0:T(8,128)(2,1)S(1)} %get-tuple-element.38), channel_id=1, source_target_pairs={{0,1},{1,0},{2,3},{3,2},{4,5},{5,4},{6,7},{7,6},{8,9},{9,8},{10,11... | collective-permute-start | bytes 1474568 | tf_op jit(solution)/shard_map/ppermute | solution.py:273
  3.7 6.5 %collective-permute-start = (bf16[256,128]{1,0:T(8,128)(2,1)S(1)}, bf16[256,128]{1,0:T(8,128)(2,1)S(1)}, u32[]{:S(2)}, u32[]{:S(2)}) collective-permute-start(bf16[256,128]{1,0:T(8,128)(2,1)S(1)} %get-tuple-element.33), channel_id=1, source_target_pairs={{4,2},{8,6},{12,10},{16,14},{20,18},{24,22},{28,26},{2,4},{6,8},{1... | collective-permute-start | bytes 196616 | tf_op jit(solution)/shard_map/ppermute | solution.py:265
  6.2 4.0 %collective-permute-start.1 = (bf16[256,128]{1,0:T(8,128)(2,1)S(1)}, bf16[256,128]{1,0:T(8,128)(2,1)S(1)}, u32[]{:S(2)}, u32[]{:S(2)}) collective-permute-start(bf16[256,128]{1,0:T(8,128)(2,1)S(1)} %get-tuple-element.34), channel_id=1, source_target_pairs={{2,0},{6,4},{10,8},{14,12},{18,16},{22,20},{26,24},{30,28},{0,2},{... | collective-permute-start | bytes 196616 | tf_op jit(solution)/shard_map/ppermute | solution.py:265
  10.8 6.5 %collective-permute-start.4 = (bf16[128,256]{1,0:T(8,128)(2,1)S(1)}, bf16[128,256]{1,0:T(8,128)(2,1)S(1)}, u32[]{:S(2)}, u32[]{:S(2)}) collective-permute-start(bf16[128,256]{1,0:T(8,128)(2,1)S(1)} %get-tuple-element.43), channel_id=1, source_target_pairs={{4,2},{8,6},{12,10},{16,14},{20,18},{24,22},{28,26},{2,4},{6,8},{1... | collective-permute-start | bytes 196616 | tf_op jit(solution)/shard_map/ppermute | solution.py:265
  13.4 5.9 %collective-permute-start.3 = (bf16[256,256]{1,0:T(8,128)(2,1)S(1)}, bf16[256,256]{1,0:T(8,128)(2,1)S(1)}, u32[]{:S(2)}, u32[]{:S(2)}) collective-permute-start(bf16[256,256]{1,0:T(8,128)(2,1)S(1)} %get-tuple-element.35.fit), channel_id=1, source_target_pairs={{0,1},{1,0},{2,3},{3,2},{4,5},{5,4},{6,7},{7,6},{8,9},{9,8},{10,11... | collective-permute-start | bytes 393224 | tf_op jit(solution)/shard_map/ppermute | solution.py:276
  14.0 3.3 %collective-permute-start.5 = (bf16[128,256]{1,0:T(8,128)(2,1)S(1)}, bf16[128,256]{1,0:T(8,128)(2,1)S(1)}, u32[]{:S(2)}, u32[]{:S(2)}) collective-permute-start(bf16[128,256]{1,0:T(8,128)(2,1)S(1)} %get-tuple-element.44), channel_id=1, source_target_pairs={{2,0},{6,4},{10,8},{14,12},{18,16},{22,20},{26,24},{30,28},{0,2},{... | collective-permute-start | bytes 196616 | tf_op jit(solution)/shard_map/ppermute | solution.py:265
  17.5 4.3 %collective-permute-start.6 = (bf16[128,256]{1,0:T(8,128)(2,1)S(1)}, bf16[128,256]{1,0:T(8,128)(2,1)S(1)}, u32[]{:S(2)}, u32[]{:S(2)}) collective-permute-start(bf16[128,256]{1,0:T(8,128)(2,1)S(1)} %get-tuple-element.46), channel_id=1, source_target_pairs={{0,1},{1,0},{2,3},{3,2},{4,5},{5,4},{6,7},{7,6},{8,9},{9,8},{10,11... | collective-permute-start | bytes 196616 | tf_op jit(solution)/shard_map/ppermute | solution.py:295

commit v3 on v2

--- a/solution.py
+++ b/solution.py
@@ -107,8 +107,8 @@
     return jnp.where(odd, near, far), jnp.where(odd, far, near)
 
 
-def rim_kernel(voxels, live, movie, foot, start, far, near, count, *rest):
-    numbers, rims, traces, edge, middle, sems = rest[-6:]
+def rim_kernel(voxels, live, movie, foot, start, far, near, count, traces, *rest):
+    numbers, rims, edge, middle, sems = rest[-5:]
     rim = edge.shape[1]
     frames = edge.shape[0]
     there = 1 - lax.axis_index("tm")
@@ -121,7 +121,7 @@
         copied(movie.at[:, pl.ds(voxels // 2, rim)], middle, sems.at[5]),
     ]
     large = []
-    if len(rest) > 6:
+    if len(rest) > 5:
         first = first_column(there, voxels, rim)
         for i in range(voxels // 2 // rim - 1):
             column = movie.at[:, pl.ds(pl.multiple_of(first + i * rim, 128), rim)]
@@ -141,17 +141,27 @@
         copy.wait()
 
 
-def drive_kernel(voxels, count, movie, foot, start, plan, scale, cross_high, cross_low, rims, flat, masked):
+def drive_kernel(
+    voxels, count, movie, foot, start, plan, scale, cross_high, cross_low, rims, flat, masked, shown, sems
+):
     rim = foot.shape[0] - voxels
+    step = voxels // 2
+    loads = []
+    for i in range(2):
+        columns = pl.ds(i * step, step)
+        loads.append(copied(movie.at[:, columns], shown.at[:, columns], sems.at[i]))
     alive = count[0:1]
     masked[:voxels] = living(alive, foot[:voxels])
     ends = living(alive, foot[voxels:])
     masked[voxels:] = jnp.where(at_end("slab"), jnp.zeros_like(ends), ends)
     rims[:rim] = -masked[:rim]
     rims[rim:] = masked[voxels:]
-    flat[...] = movie[:, :rim].T
-    drive = mm(movie[...], masked[:voxels])
     gram = t_mm(masked[...], masked[...])
+    loads[0].wait()
+    flat[...] = shown[:, :rim].T
+    drive = mm(shown[:, :step], masked[:step])
+    loads[1].wait()
+    drive = drive + mm(shown[:, step:], masked[step:voxels])
     inverse = 1.0 / (diagonal(gram) + 1e-06)
     scale[...] = jnp.broadcast_to(inverse, scale.shape)
     gram_high, gram_low = halves(gram)
@@ -352,21 +362,21 @@
         pltpu.with_memory_space_constraint(x, pltpu.HBM)
         for x in (live_count, recording, footprints, traces)
     ]
-    far, near, count, *outgoing = call(
+    far, near, count, begun, *outgoing = call(
         functools.partial(rim_kernel, voxels),
         [
             pltpu.VMEM((frames, rim), BF),
             pltpu.VMEM((frames, rim), BF),
             pltpu.VMEM((8, neurons), jnp.int32),
+            pltpu.VMEM((frames, neurons), F32),
         ]
         + share_shape,
         [LEFT_THERE] * 4,
-        [WHOLE] * (3 + len(share_shape)),
+        [WHOLE] * (4 + len(share_shape)),
         1.5,
         scratch_shapes=[
             pltpu.SMEM(live_count.shape, jnp.int32),
             pltpu.VMEM((2 * rim, neurons), BF),
-            pltpu.VMEM((frames, neurons), F32),
             pltpu.VMEM((frames, rim), BF),
             pltpu.VMEM((frames, rim), BF),
             COPIES((6 + main,)),
@@ -374,7 +384,7 @@
     )(*pinned)
     far = swapped(far, 1)
     near = swapped(near, 0)
-    plan, scale, cross_high, cross_low, rims, flat, masked = call(
+    plan, scale, cross_high, cross_low, rims, flat, masked, shown = call(
         functools.partial(drive_kernel, voxels),
         [
             shape((frames, neurons), F32),
@@ -384,11 +394,13 @@
             shape((2 * rim, neurons), BF),
             shape((rim, frames), BF),
             pltpu.VMEM((extended, neurons), BF),
+            pltpu.VMEM((frames, voxels), BF),
         ],
-        [WHOLE] * 4,
-        [WHOLE] * 7,
-        1.2,
-    )(count, recording, footprints, traces)
+        [WHOLE, LEFT_THERE, WHOLE, WHOLE],
+        [WHOLE] * 8,
+        1.6,
+        scratch_shapes=[COPIES((2,))],
+    )(count, pinned[1], footprints, begun)
     new_tr, rounded, far, near = call(
         sweep_kernel,
         [
@@ -402,7 +414,7 @@
         0.5,
     )(plan, scale, cross_high, cross_low, rims, flat, far, near)
     if split:
-        return halved(voxels, rim, masked, recording, flat, outgoing[0], new_tr, rounded, far, near)
+        return halved(voxels, rim, masked, shown, flat, outgoing[0], new_tr, rounded, far, near)
     return new_tr, spread(voxels, rim, masked, recording, rounded)
 
 

time: 22.7 us -> 22.6 us (level)
  waiting for transfers between devices: 6.54 us -> 5.7 us
  Pallas kernels: 6.33 us -> 7.12 us
    pallas_call x1, Pallas kernels: 1.23 us -> 2.08 us  [on_device(): call(functools.partial(drive_kernel, voxels), [shape((frames, neurons), F...]
    ppermute x4, waiting for transfers between devices: 4.35 us -> 3.51 us  [swapped(): return lax.ppermute(block, 'slab', [(j, i) for i, j in route] + route)]
  transfers between devices with their start and end apart: 7 -> 7, of which waited for: 4 -> 4; matrix products, arithmetic and copies ran while one was open for 0% -> 0% of each run, Pallas kernels for 18% -> 22%
where the time goes in v3:
time: 22.6 us; the launch traced here: 22.4 us
  starting transfers between devices  8.9 us (39%)
  Pallas kernels  7.12 us (32%)
  waiting for transfers between devices  5.7 us (25%)
  between operations  0.7 us (3%)
    ppermute x4, starting transfers between devices, swapped(): return lax.ppermute(block, 'slab', [(j, i) for i, j in route] + route)  6.14 us
    ppermute x4, waiting for transfers between devices, swapped(): return lax.ppermute(block, 'slab', [(j, i) for i, j in route] + route)  3.51 us
    pallas_call x1, Pallas kernels, on_device(): call(functools.partial(drive_kernel, voxels), [shape((frames, neurons), F...  2.08 us
    ppermute x1, starting transfers between devices, halved(): movie = lax.ppermute(outgoing, 'tm', across)  1.56 us
    pallas_call x1, Pallas kernels, halved(): call(functools.partial(main_kernel, voxels, rim), [pltpu.HBM((share, neur...  1.53 us
    pallas_call x1, Pallas kernels, on_device(): call(functools.partial(rim_kernel, voxels), [pltpu.VMEM((frames, rim), BF...  1.46 us
    ppermute x1, waiting for transfers between devices, halved(): other = lax.ppermute(rounded, 'tm', across)  1.14 us
    ppermute x1, waiting for transfers between devices, halved(): came = lax.ppermute(sent, 'tm', across)  1.05 us
  transfers between devices with their start and end apart: 7, of which 4 were waited for; matrix products, arithmetic and copies ran while one was open for 0% of the time, Pallas kernels for 22%

profile of v3, /device:TPU:24, one launch (start us, length us, event | category | flops | bytes accessed | tf_op | source)
XLA Modules:
  0.0 22.4 jit_solution(6644315642941876659)
XLA Ops:
  0.6 0.0 copy-start
  0.6 1.5 %shard_map.59 = (bf16[256,128]{1,0:T(8,128)(2,1)S(1)}, bf16[256,128]{1,0:T(8,128)(2,1)S(1)}, s32[8,256]{1,0:T(8,128)S(1)}, f32[256,256]{1,0:T(8,128)S(1)}, bf16[1920,128]{1,0:T(8,128)(2,1)S(1)}) custom-call(s32[16]{0:T(128)} %live.1, bf16[256,2048]{1,0:T(8,128)(2,1)} %movie.3, bf16[2176,256]{1,0:T(8,128)(2,1)} %foot.3, f32[256,256]{1,0:T(8,128)} %start.1), custom_call_target="tpu_custom_call" | custom-call | bytes 5535000 | tf_op jit(solution)/shard_map/pallas_call | solution.py:365
  2.1 1.6 %collective-permute-start.2 = (bf16[1920,128]{1,0:T(8,128)(2,1)S(1)}, bf16[1920,128]{1,0:T(8,128)(2,1)S(1)}, u32[]{:S(2)}, u32[]{:S(2)}) collective-permute-start(bf16[1920,128]{1,0:T(8,128)(2,1)S(1)} %get-tuple-element.42), channel_id=1, source_target_pairs={{0,1},{1,0},{2,3},{3,2},{4,5},{5,4},{6,7},{7,6},{8,9},{9,8},{10,11... | collective-permute-start | bytes 1474568 | tf_op jit(solution)/shard_map/ppermute | solution.py:283
  3.7 2.5 %collective-permute-start = (bf16[256,128]{1,0:T(8,128)(2,1)S(1)}, bf16[256,128]{1,0:T(8,128)(2,1)S(1)}, u32[]{:S(2)}, u32[]{:S(2)}) collective-permute-start(bf16[256,128]{1,0:T(8,128)(2,1)S(1)} %get-tuple-element.37), channel_id=1, source_target_pairs={{4,2},{8,6},{12,10},{16,14},{20,18},{24,22},{28,26},{2,4},{6,8},{1... | collective-permute-start | bytes 196616 | tf_op jit(solution)/shard_map/ppermute | solution.py:275
  6.1 1.1 %collective-permute-start.1 = (bf16[256,128]{1,0:T(8,128)(2,1)S(1)}, bf16[256,128]{1,0:T(8,128)(2,1)S(1)}, u32[]{:S(2)}, u32[]{:S(2)}) collective-permute-start(bf16[256,128]{1,0:T(8,128)(2,1)S(1)} %get-tuple-element.38), channel_id=1, source_target_pairs={{2,0},{6,4},{10,8},{14,12},{18,16},{22,20},{26,24},{30,28},{0,2},{... | collective-permute-start | bytes 196616 | tf_op jit(solution)/shard_map/ppermute | solution.py:275
  7.3 0.0 copy-done
  7.3 2.1 %shard_map.60 = (f32[256,256]{1,0:T(8,128)S(1)}, f32[8,256]{1,0:T(8,128)S(1)}, bf16[128,128]{1,0:T(8,128)(2,1)S(1)}, bf16[128,128]{1,0:T(8,128)(2,1)S(1)}, bf16[...) custom-call(s32[8,256]{1,0:T(8,128)S(1)} %get-tuple-element.27.count, ...), custom_call_target="tpu_custom_call" | custom-call | bytes 5904000 | tf_op jit(solution)/shard_map/pallas_call | solution.py:387
  9.4 0.8 %collective-permute-done.far = bf16[256,128]{1,0:T(8,128)(2,1)S(1)} collective-permute-done((bf16[256,128]{1,0:T(8,128)(2,1)S(1)}, bf16[256,128]{1,0:T(8,128)(2,1)S(1)}, u32[]{:S(2)}, u32[]{:S(2)}) %collective-permute-start) | collective-permute-done | bytes 65568 | tf_op jit(solution)/shard_map/ppermute | solution.py:275
  10.1 0.0 collective-permute-done.1.near
  10.1 0.6 %shard_map.61 = (f32[256,256]{1,0:T(8,128)S(1)}, bf16[256,256]{1,0:T(8,128)(2,1)S(1)}, bf16[128,256]{1,0:T(8,128)(2,1)S(1)}, bf16[128,256]{1,0:T(8,128)(2,1)S(1)}) custom-call(f32[256,256]{1,0:T(8,128)S(1)} %get-tuple-element.31.plan, f32[8,256]{1,0:T(8,128)S(1)} %get-tuple-element.32.scale, bf16[128,128]{1,0:T(8,128)(2,1)S(1)} %get-tuple-element.33.cross_high, ...), custom_call_target="tpu_custom_call" | custom-call | bytes 1845000 | tf_op jit(solution)/shard_map/pallas_call | solution.py:404
  10.7 2.5 %collective-permute-start.4 = (bf16[128,256]{1,0:T(8,128)(2,1)S(1)}, bf16[128,256]{1,0:T(8,128)(2,1)S(1)}, u32[]{:S(2)}, u32[]{:S(2)}) collective-permute-start(bf16[128,256]{1,0:T(8,128)(2,1)S(1)} %get-tuple-element.47), channel_id=1, source_target_pairs={{4,2},{8,6},{12,10},{16,14},{20,18},{24,22},{28,26},{2,4},{6,8},{1... | collective-permute-start | bytes 196616 | tf_op jit(solution)/shard_map/ppermute | solution.py:275
  13.3 0.6 %collective-permute-start.3 = (bf16[256,256]{1,0:T(8,128)(2,1)S(1)}, bf16[256,256]{1,0:T(8,128)(2,1)S(1)}, u32[]{:S(2)}, u32[]{:S(2)}) collective-permute-start(bf16[256,256]{1,0:T(8,128)(2,1)S(1)} %get-tuple-element.39.fit), channel_id=1, source_target_pairs={{0,1},{1,0},{2,3},{3,2},{4,5},{5,4},{6,7},{7,6},{8,9},{9,8},{10,11... | collective-permute-start | bytes 393224 | tf_op jit(solution)/shard_map/ppermute | solution.py:286
  13.9 0.0 collective-permute-start.5
  13.9 0.6 %shard_map.62 = (f32[1024,256]{1,0:T(8,128)S(1)}, f32[256,256]{1,0:T(8,128)S(1)}, f32[256,256]{1,0:T(8,128)S(1)}) custom-call(bf16[256,2048]{1,0:T(8,128)(2,1)S(1)} %get-tuple-element.30.movie, bf16[2176,256]{1,0:T(8,128)(2,1)S(1)} %get-tuple-element.29.foot, bf16[256,256]{1,0:T(8,128)(2,1)S(1)} %get-tuple-element.39.fit, ...), custom_call_target="tpu_custom_call" | custom-call | bytes 2214000 | tf_op jit(solution)/shard_map/pallas_call | solution.py:287
  14.5 2.7 %collective-permute-done.4.far = bf16[128,256]{1,0:T(8,128)(2,1)S(1)} collective-permute-done((bf16[128,256]{1,0:T(8,128)(2,1)S(1)}, bf16[128,256]{1,0:T(8,128)(2,1)S(1)}, u32[]{:S(2)}, u32[]{:S(2)}) %collective-permute-start.4) | collective-permute-done | bytes 65568 | tf_op jit(solution)/shard_map/ppermute | solution.py:275
  17.2 0.0 collective-permute-done.5.near
  17.2 0.2 shard_map.64
  17.4 0.6 %collective-permute-start.6 = (bf16[128,256]{1,0:T(8,128)(2,1)S(1)}, bf16[128,256]{1,0:T(8,128)(2,1)S(1)}, u32[]{:S(2)}, u32[]{:S(2)}) collective-permute-start(bf16[128,256]{1,0:T(8,128)(2,1)S(1)} %get-tuple-element.50), channel_id=1, source_target_pairs={{0,1},{1,0},{2,3},{3,2},{4,5},{5,4},{6,7},{7,6},{8,9},{9,8},{10,11... | collective-permute-start | bytes 196616 | tf_op jit(solution)/shard_map/ppermute | solution.py:305
  18.0 1.1 %collective-permute-done.3.fit = bf16[256,256]{1,0:T(8,128)(2,1)S(1)} collective-permute-done((bf16[256,256]{1,0:T(8,128)(2,1)S(1)}, bf16[256,256]{1,0:T(8,128)(2,1)S(1)}, u32[]{:S(2)}, u32[]{:S(2)}) %collective-permute-start.3) | collective-permute-done | bytes 131104 | tf_op jit(solution)/shard_map/ppermute | solution.py:286
  19.2 0.0 collective-permute-done.2.movie
  19.2 1.5 %shard_map.63 = (bf16[1088,256]{1,0:T(8,128)(2,1)}, f32[256,256]{1,0:T(8,128)}, f32[8,256]{1,0:T(8,128)S(1)}) custom-call(bf16[2176,256]{1,0:T(8,128)(2,1)S(1)} %get-tuple-element.29.foot, f32[1024,256]{1,0:T(8,128)S(1)} %get-tuple-element.40.total, f32[256,256]{1,0:T(8,128)S(1)} %get-tuple-element.41.quad, ...), custom_call_target="tpu_custom_call" | custom-call | bytes 7380000 | tf_op jit(solution)/shard_map/pallas_call | solution.py:306
  20.7 1.1 %collective-permute-done.6.came = bf16[128,256]{1,0:T(8,128)(2,1)S(1)} collective-permute-done((bf16[128,256]{1,0:T(8,128)(2,1)S(1)}, bf16[128,256]{1,0:T(8,128)(2,1)S(1)}, u32[]{:S(2)}, u32[]{:S(2)}) %collective-permute-start.6) | collective-permute-done | bytes 65568 | tf_op jit(solution)/shard_map/ppermute | solution.py:305
  21.8 0.7 %shard_map.65 = bf16[1088,256]{1,0:T(8,128)(2,1)} custom-call(bf16[1088,256]{1,0:T(8,128)(2,1)} %get-tuple-element.45.sofar, bf16[2176,256]{1,0:T(8,128)(2,1)S(1)} %get-tuple-element.29.foot, f32[128,256]{1,0:T(8,128)S(1)} %get-tuple-element.49.lead, bf16[128,256]{1,0:T(8,128)(2,1)S(1)} %collective-permute-done.6.came, ...), custom_call_target="tpu_custom_call", output_to_operand_aliasing={{}: (0, {})} | custom-call | bytes 2952000 | tf_op jit(solution)/shard_map/pallas_call | solution.py:314
Async XLA Ops:
  0.6 6.6 %copy-start = (bf16[2176,256]{1,0:T(8,128)(2,1)S(1)}, bf16[2176,256]{1,0:T(8,128)(2,1)}, u32[]{:S(2)}) copy-start(bf16[2176,256]{1,0:T(8,128)(2,1)} %foot.3) | copy-start | bytes 3342340
  2.1 17.1 %collective-permute-start.2 = (bf16[1920,128]{1,0:T(8,128)(2,1)S(1)}, bf16[1920,128]{1,0:T(8,128)(2,1)S(1)}, u32[]{:S(2)}, u32[]{:S(2)}) collective-permute-start(bf16[1920,128]{1,0:T(8,128)(2,1)S(1)} %get-tuple-element.42), channel_id=1, source_target_pairs={{0,1},{1,0},{2,3},{3,2},{4,5},{5,4},{6,7},{7,6},{8,9},{9,8},{10,11... | collective-permute-start | bytes 1474568 | tf_op jit(solution)/shard_map/ppermute | solution.py:283
  3.7 6.5 %collective-permute-start = (bf16[256,128]{1,0:T(8,128)(2,1)S(1)}, bf16[256,128]{1,0:T(8,128)(2,1)S(1)}, u32[]{:S(2)}, u32[]{:S(2)}) collective-permute-start(bf16[256,128]{1,0:T(8,128)(2,1)S(1)} %get-tuple-element.37), channel_id=1, source_target_pairs={{4,2},{8,6},{12,10},{16,14},{20,18},{24,22},{28,26},{2,4},{6,8},{1... | collective-permute-start | bytes 196616 | tf_op jit(solution)/shard_map/ppermute | solution.py:275
  6.1 4.0 %collective-permute-start.1 = (bf16[256,128]{1,0:T(8,128)(2,1)S(1)}, bf16[256,128]{1,0:T(8,128)(2,1)S(1)}, u32[]{:S(2)}, u32[]{:S(2)}) collective-permute-start(bf16[256,128]{1,0:T(8,128)(2,1)S(1)} %get-tuple-element.38), channel_id=1, source_target_pairs={{2,0},{6,4},{10,8},{14,12},{18,16},{22,20},{26,24},{30,28},{0,2},{... | collective-permute-start | bytes 196616 | tf_op jit(solution)/shard_map/ppermute | solution.py:275
  10.7 6.5 %collective-permute-start.4 = (bf16[128,256]{1,0:T(8,128)(2,1)S(1)}, bf16[128,256]{1,0:T(8,128)(2,1)S(1)}, u32[]{:S(2)}, u32[]{:S(2)}) collective-permute-start(bf16[128,256]{1,0:T(8,128)(2,1)S(1)} %get-tuple-element.47), channel_id=1, source_target_pairs={{4,2},{8,6},{12,10},{16,14},{20,18},{24,22},{28,26},{2,4},{6,8},{1... | collective-permute-start | bytes 196616 | tf_op jit(solution)/shard_map/ppermute | solution.py:275
  13.3 5.9 %collective-permute-start.3 = (bf16[256,256]{1,0:T(8,128)(2,1)S(1)}, bf16[256,256]{1,0:T(8,128)(2,1)S(1)}, u32[]{:S(2)}, u32[]{:S(2)}) collective-permute-start(bf16[256,256]{1,0:T(8,128)(2,1)S(1)} %get-tuple-element.39.fit), channel_id=1, source_target_pairs={{0,1},{1,0},{2,3},{3,2},{4,5},{5,4},{6,7},{7,6},{8,9},{9,8},{10,11... | collective-permute-start | bytes 393224 | tf_op jit(solution)/shard_map/ppermute | solution.py:286
  13.9 3.3 %collective-permute-start.5 = (bf16[128,256]{1,0:T(8,128)(2,1)S(1)}, bf16[128,256]{1,0:T(8,128)(2,1)S(1)}, u32[]{:S(2)}, u32[]{:S(2)}) collective-permute-start(bf16[128,256]{1,0:T(8,128)(2,1)S(1)} %get-tuple-element.48), channel_id=1, source_target_pairs={{2,0},{6,4},{10,8},{14,12},{18,16},{22,20},{26,24},{30,28},{0,2},{... | collective-permute-start | bytes 196616 | tf_op jit(solution)/shard_map/ppermute | solution.py:275
  17.4 4.3 %collective-permute-start.6 = (bf16[128,256]{1,0:T(8,128)(2,1)S(1)}, bf16[128,256]{1,0:T(8,128)(2,1)S(1)}, u32[]{:S(2)}, u32[]{:S(2)}) collective-permute-start(bf16[128,256]{1,0:T(8,128)(2,1)S(1)} %get-tuple-element.50), channel_id=1, source_target_pairs={{0,1},{1,0},{2,3},{3,2},{4,5},{5,4},{6,7},{7,6},{8,9},{9,8},{10,11... | collective-permute-start | bytes 196616 | tf_op jit(solution)/shard_map/ppermute | solution.py:305

commit v4 on v3

--- a/solution.py
+++ b/solution.py
@@ -130,11 +130,12 @@
         copy.wait()
     alive = numbers[lax.axis_index("slab")]
     count[...] = jnp.full(count.shape, alive, jnp.int32)
-    seen = mm_t(living(alive, traces[...]).astype(BF), rims[...])
+    high, low = halves(living(alive, traces[...]))
+    seen = mm_t(high, rims[...]) + mm_t(low, rims[...])
     backward = edge[...].astype(F32) - seen[:, :rim]
     one, two = for_near_and_far(seen[:, rim:], backward)
-    near[...] = one.astype(BF)
-    far[...] = two.astype(BF)
+    near[...] = one
+    far[...] = two
     if large:
         rest[0][(voxels // 2 // rim - 1) * frames:] = packed(there, middle[...])
     for copy in large:
@@ -182,7 +183,8 @@
     rim = flat.shape[0]
     edges = rims[...]
     beside = jnp.concatenate(from_prev_and_next(near[...], far[...]), axis=1)
-    stepped = plan[...] + mm(beside, edges) * scale[0:1]
+    high, low = halves(beside)
+    stepped = plan[...] + (mm(high, edges) + mm(low, edges)) * scale[0:1]
     first = jnp.maximum(stepped[:, :GROUP], 0.0)
     high, low = halves(first)
     cross = cross_high[...]
@@ -365,8 +367,8 @@
     far, near, count, begun, *outgoing = call(
         functools.partial(rim_kernel, voxels),
         [
-            pltpu.VMEM((frames, rim), BF),
-            pltpu.VMEM((frames, rim), BF),
+            pltpu.VMEM((frames, rim), F32),
+            pltpu.VMEM((frames, rim), F32),
             pltpu.VMEM((8, neurons), jnp.int32),
             pltpu.VMEM((frames, neurons), F32),
         ]

time: 22.6 us -> 24.1 us (1.066)
  waiting for transfers between devices: 5.7 us -> 7 us
    ppermute x4, waiting for transfers between devices: 3.51 us -> 4.49 us  [swapped(): return lax.ppermute(block, 'slab', [(j, i) for i, j in route] + route)]
    ppermute x1, waiting for transfers between devices: 1.05 us -> 1.89 us  [halved(): came = lax.ppermute(sent, 'tm', across)]
    ppermute x1, waiting for transfers between devices: 1.14 us -> 0.62 us  [halved(): other = lax.ppermute(rounded, 'tm', across)]
  transfers between devices with their start and end apart: 7 -> 7, of which waited for: 4 -> 4; matrix products, arithmetic and copies ran while one was open for 0% -> 0% of each run, Pallas kernels for 22% -> 21%
where the time goes in v4:
time: 24.1 us; the launch traced here: 23.8 us
  starting transfers between devices  8.82 us (37%)
  Pallas kernels  7.26 us (30%)
  waiting for transfers between devices  7 us (29%)
  between operations  0.7 us (3%)
    ppermute x4, starting transfers between devices, swapped(): return lax.ppermute(block, 'slab', [(j, i) for i, j in route] + route)  6.07 us
    ppermute x4, waiting for transfers between devices, swapped(): return lax.ppermute(block, 'slab', [(j, i) for i, j in route] + route)  4.49 us
    pallas_call x1, Pallas kernels, on_device(): call(functools.partial(drive_kernel, voxels), [shape((frames, neurons), F...  2.07 us
    ppermute x1, waiting for transfers between devices, halved(): came = lax.ppermute(sent, 'tm', across)  1.89 us
    ppermute x1, starting transfers between devices, halved(): movie = lax.ppermute(outgoing, 'tm', across)  1.56 us
    pallas_call x1, Pallas kernels, halved(): call(functools.partial(main_kernel, voxels, rim), [pltpu.HBM((share, neur...  1.53 us
    pallas_call x1, Pallas kernels, on_device(): call(functools.partial(rim_kernel, voxels), [pltpu.VMEM((frames, rim), F3...  1.52 us
    pallas_call x1, Pallas kernels, halved(): call(functools.partial(edge_kernel, voxels), pltpu.HBM((share, neurons),...  0.67 us
  transfers between devices with their start and end apart: 7, of which 4 were waited for; matrix products, arithmetic and copies ran while one was open for 0% of the time, Pallas kernels for 21%

profile of v4, /device:TPU:24, one launch (start us, length us, event | category | flops | bytes accessed | tf_op | source)
XLA Modules:
  0.0 23.8 jit_solution(18406998620813788481)
XLA Ops:
  0.6 0.0 copy-start
  0.6 1.5 %shard_map.59 = (f32[256,128]{1,0:T(8,128)S(1)}, f32[256,128]{1,0:T(8,128)S(1)}, s32[8,256]{1,0:T(8,128)S(1)}, f32[256,256]{1,0:T(8,128)S(1)}, bf16[1920,128]{1,0:T(8,128)(2,1)S(1)}) custom-call(s32[16]{0:T(128)} %live.1, bf16[256,2048]{1,0:T(8,128)(2,1)} %movie.3, bf16[2176,256]{1,0:T(8,128)(2,1)} %foot.3, f32[256,256]{1,0:T(8,128)} %start.1), custom_call_target="tpu_custom_call" | custom-call | bytes 5535000 | tf_op jit(solution)/shard_map/pallas_call | solution.py:367
  2.2 1.6 %collective-permute-start.2 = (bf16[1920,128]{1,0:T(8,128)(2,1)S(1)}, bf16[1920,128]{1,0:T(8,128)(2,1)S(1)}, u32[]{:S(2)}, u32[]{:S(2)}) collective-permute-start(bf16[1920,128]{1,0:T(8,128)(2,1)S(1)} %get-tuple-element.42), channel_id=1, source_target_pairs={{0,1},{1,0},{2,3},{3,2},{4,5},{5,4},{6,7},{7,6},{8,9},{9,8},{10,11... | collective-permute-start | bytes 1474568 | tf_op jit(solution)/shard_map/ppermute | solution.py:285
  3.7 2.5 %collective-permute-start = (f32[256,128]{1,0:T(8,128)S(1)}, f32[256,128]{1,0:T(8,128)S(1)}, u32[]{:S(2)}, u32[]{:S(2)}) collective-permute-start(f32[256,128]{1,0:T(8,128)S(1)} %get-tuple-element.37), channel_id=1, source_target_pairs={{4,2},{8,6},{12,10},{16,14},{20,18},{24,22},{28,26},{2,4},{6,8},{1... | collective-permute-start | bytes 393224 | tf_op jit(solution)/shard_map/ppermute | solution.py:277
  6.2 1.1 %collective-permute-start.1 = (f32[256,128]{1,0:T(8,128)S(1)}, f32[256,128]{1,0:T(8,128)S(1)}, u32[]{:S(2)}, u32[]{:S(2)}) collective-permute-start(f32[256,128]{1,0:T(8,128)S(1)} %get-tuple-element.38), channel_id=1, source_target_pairs={{2,0},{6,4},{10,8},{14,12},{18,16},{22,20},{26,24},{30,28},{0,2},{... | collective-permute-start | bytes 393224 | tf_op jit(solution)/shard_map/ppermute | solution.py:277
  7.3 0.0 copy-done
  7.3 2.1 %shard_map.60 = (f32[256,256]{1,0:T(8,128)S(1)}, f32[8,256]{1,0:T(8,128)S(1)}, bf16[128,128]{1,0:T(8,128)(2,1)S(1)}, bf16[128,128]{1,0:T(8,128)(2,1)S(1)}, bf16[...) custom-call(s32[8,256]{1,0:T(8,128)S(1)} %get-tuple-element.27.count, ...), custom_call_target="tpu_custom_call" | custom-call | bytes 5904000 | tf_op jit(solution)/shard_map/pallas_call | solution.py:389
  9.4 1.6 %collective-permute-done.far = f32[256,128]{1,0:T(8,128)S(1)} collective-permute-done((f32[256,128]{1,0:T(8,128)S(1)}, f32[256,128]{1,0:T(8,128)S(1)}, u32[]{:S(2)}, u32[]{:S(2)}) %collective-permute-start) | collective-permute-done | bytes 131104 | tf_op jit(solution)/shard_map/ppermute | solution.py:277
  11.0 0.0 collective-permute-done.1.near
  11.0 0.7 %shard_map.61 = (f32[256,256]{1,0:T(8,128)S(1)}, bf16[256,256]{1,0:T(8,128)(2,1)S(1)}, bf16[128,256]{1,0:T(8,128)(2,1)S(1)}, bf16[128,256]{1,0:T(8,128)(2,1)S(1)}) custom-call(f32[256,256]{1,0:T(8,128)S(1)} %get-tuple-element.31.plan, f32[8,256]{1,0:T(8,128)S(1)} %get-tuple-element.32.scale, bf16[128,128]{1,0:T(8,128)(2,1)S(1)} %get-tuple-element.33.cross_high, ...), custom_call_target="tpu_custom_call" | custom-call | bytes 1845000 | tf_op jit(solution)/shard_map/pallas_call | solution.py:406
  11.7 2.5 %collective-permute-start.4 = (bf16[128,256]{1,0:T(8,128)(2,1)S(1)}, bf16[128,256]{1,0:T(8,128)(2,1)S(1)}, u32[]{:S(2)}, u32[]{:S(2)}) collective-permute-start(bf16[128,256]{1,0:T(8,128)(2,1)S(1)} %get-tuple-element.47), channel_id=1, source_target_pairs={{4,2},{8,6},{12,10},{16,14},{20,18},{24,22},{28,26},{2,4},{6,8},{1... | collective-permute-start | bytes 196616 | tf_op jit(solution)/shard_map/ppermute | solution.py:277
  14.2 0.6 %collective-permute-start.3 = (bf16[256,256]{1,0:T(8,128)(2,1)S(1)}, bf16[256,256]{1,0:T(8,128)(2,1)S(1)}, u32[]{:S(2)}, u32[]{:S(2)}) collective-permute-start(bf16[256,256]{1,0:T(8,128)(2,1)S(1)} %get-tuple-element.39.fit), channel_id=1, source_target_pairs={{0,1},{1,0},{2,3},{3,2},{4,5},{5,4},{6,7},{7,6},{8,9},{9,8},{10,11... | collective-permute-start | bytes 393224 | tf_op jit(solution)/shard_map/ppermute | solution.py:288
  14.8 0.0 collective-permute-start.5
  14.8 0.6 %shard_map.62 = (f32[1024,256]{1,0:T(8,128)S(1)}, f32[256,256]{1,0:T(8,128)S(1)}, f32[256,256]{1,0:T(8,128)S(1)}) custom-call(bf16[256,2048]{1,0:T(8,128)(2,1)S(1)} %get-tuple-element.30.movie, bf16[2176,256]{1,0:T(8,128)(2,1)S(1)} %get-tuple-element.29.foot, bf16[256,256]{1,0:T(8,128)(2,1)S(1)} %get-tuple-element.39.fit, ...), custom_call_target="tpu_custom_call" | custom-call | bytes 2214000 | tf_op jit(solution)/shard_map/pallas_call | solution.py:289
  15.4 2.9 %collective-permute-done.4.far = bf16[128,256]{1,0:T(8,128)(2,1)S(1)} collective-permute-done((bf16[128,256]{1,0:T(8,128)(2,1)S(1)}, bf16[128,256]{1,0:T(8,128)(2,1)S(1)}, u32[]{:S(2)}, u32[]{:S(2)}) %collective-permute-start.4) | collective-permute-done | bytes 65568 | tf_op jit(solution)/shard_map/ppermute | solution.py:277
  18.3 0.0 collective-permute-done.5.near
  18.3 0.2 shard_map.64
  18.5 0.6 %collective-permute-start.6 = (bf16[128,256]{1,0:T(8,128)(2,1)S(1)}, bf16[128,256]{1,0:T(8,128)(2,1)S(1)}, u32[]{:S(2)}, u32[]{:S(2)}) collective-permute-start(bf16[128,256]{1,0:T(8,128)(2,1)S(1)} %get-tuple-element.50), channel_id=1, source_target_pairs={{0,1},{1,0},{2,3},{3,2},{4,5},{5,4},{6,7},{7,6},{8,9},{9,8},{10,11... | collective-permute-start | bytes 196616 | tf_op jit(solution)/shard_map/ppermute | solution.py:307
  19.1 0.6 %collective-permute-done.3.fit = bf16[256,256]{1,0:T(8,128)(2,1)S(1)} collective-permute-done((bf16[256,256]{1,0:T(8,128)(2,1)S(1)}, bf16[256,256]{1,0:T(8,128)(2,1)S(1)}, u32[]{:S(2)}, u32[]{:S(2)}) %collective-permute-start.3) | collective-permute-done | bytes 131104 | tf_op jit(solution)/shard_map/ppermute | solution.py:288
  19.7 0.0 collective-permute-done.2.movie
  19.7 1.5 %shard_map.63 = (bf16[1088,256]{1,0:T(8,128)(2,1)}, f32[256,256]{1,0:T(8,128)}, f32[8,256]{1,0:T(8,128)S(1)}) custom-call(bf16[2176,256]{1,0:T(8,128)(2,1)S(1)} %get-tuple-element.29.foot, f32[1024,256]{1,0:T(8,128)S(1)} %get-tuple-element.40.total, f32[256,256]{1,0:T(8,128)S(1)} %get-tuple-element.41.quad, ...), custom_call_target="tpu_custom_call" | custom-call | bytes 7380000 | tf_op jit(solution)/shard_map/pallas_call | solution.py:308
  21.2 1.9 %collective-permute-done.6.came = bf16[128,256]{1,0:T(8,128)(2,1)S(1)} collective-permute-done((bf16[128,256]{1,0:T(8,128)(2,1)S(1)}, bf16[128,256]{1,0:T(8,128)(2,1)S(1)}, u32[]{:S(2)}, u32[]{:S(2)}) %collective-permute-start.6) | collective-permute-done | bytes 65568 | tf_op jit(solution)/shard_map/ppermute | solution.py:307
  23.1 0.7 %shard_map.65 = bf16[1088,256]{1,0:T(8,128)(2,1)} custom-call(bf16[1088,256]{1,0:T(8,128)(2,1)} %get-tuple-element.45.sofar, bf16[2176,256]{1,0:T(8,128)(2,1)S(1)} %get-tuple-element.29.foot, f32[128,256]{1,0:T(8,128)S(1)} %get-tuple-element.49.lead, bf16[128,256]{1,0:T(8,128)(2,1)S(1)} %collective-permute-done.6.came, ...), custom_call_target="tpu_custom_call", output_to_operand_aliasing={{}: (0, {})} | custom-call | bytes 2952000 | tf_op jit(solution)/shard_map/pallas_call | solution.py:316
Async XLA Ops:
  0.6 6.7 %copy-start = (bf16[2176,256]{1,0:T(8,128)(2,1)S(1)}, bf16[2176,256]{1,0:T(8,128)(2,1)}, u32[]{:S(2)}) copy-start(bf16[2176,256]{1,0:T(8,128)(2,1)} %foot.3) | copy-start | bytes 3342340
  2.2 17.5 %collective-permute-start.2 = (bf16[1920,128]{1,0:T(8,128)(2,1)S(1)}, bf16[1920,128]{1,0:T(8,128)(2,1)S(1)}, u32[]{:S(2)}, u32[]{:S(2)}) collective-permute-start(bf16[1920,128]{1,0:T(8,128)(2,1)S(1)} %get-tuple-element.42), channel_id=1, source_target_pairs={{0,1},{1,0},{2,3},{3,2},{4,5},{5,4},{6,7},{7,6},{8,9},{9,8},{10,11... | collective-permute-start | bytes 1474568 | tf_op jit(solution)/shard_map/ppermute | solution.py:285
  3.7 7.3 %collective-permute-start = (f32[256,128]{1,0:T(8,128)S(1)}, f32[256,128]{1,0:T(8,128)S(1)}, u32[]{:S(2)}, u32[]{:S(2)}) collective-permute-start(f32[256,128]{1,0:T(8,128)S(1)} %get-tuple-element.37), channel_id=1, source_target_pairs={{4,2},{8,6},{12,10},{16,14},{20,18},{24,22},{28,26},{2,4},{6,8},{1... | collective-permute-start | bytes 393224 | tf_op jit(solution)/shard_map/ppermute | solution.py:277
  6.2 4.8 %collective-permute-start.1 = (f32[256,128]{1,0:T(8,128)S(1)}, f32[256,128]{1,0:T(8,128)S(1)}, u32[]{:S(2)}, u32[]{:S(2)}) collective-permute-start(f32[256,128]{1,0:T(8,128)S(1)} %get-tuple-element.38), channel_id=1, source_target_pairs={{2,0},{6,4},{10,8},{14,12},{18,16},{22,20},{26,24},{30,28},{0,2},{... | collective-permute-start | bytes 393224 | tf_op jit(solution)/shard_map/ppermute | solution.py:277
  11.7 6.6 %collective-permute-start.4 = (bf16[128,256]{1,0:T(8,128)(2,1)S(1)}, bf16[128,256]{1,0:T(8,128)(2,1)S(1)}, u32[]{:S(2)}, u32[]{:S(2)}) collective-permute-start(bf16[128,256]{1,0:T(8,128)(2,1)S(1)} %get-tuple-element.47), channel_id=1, source_target_pairs={{4,2},{8,6},{12,10},{16,14},{20,18},{24,22},{28,26},{2,4},{6,8},{1... | collective-permute-start | bytes 196616 | tf_op jit(solution)/shard_map/ppermute | solution.py:277
  14.2 5.5 %collective-permute-start.3 = (bf16[256,256]{1,0:T(8,128)(2,1)S(1)}, bf16[256,256]{1,0:T(8,128)(2,1)S(1)}, u32[]{:S(2)}, u32[]{:S(2)}) collective-permute-start(bf16[256,256]{1,0:T(8,128)(2,1)S(1)} %get-tuple-element.39.fit), channel_id=1, source_target_pairs={{0,1},{1,0},{2,3},{3,2},{4,5},{5,4},{6,7},{7,6},{8,9},{9,8},{10,11... | collective-permute-start | bytes 393224 | tf_op jit(solution)/shard_map/ppermute | solution.py:288
  14.8 3.5 %collective-permute-start.5 = (bf16[128,256]{1,0:T(8,128)(2,1)S(1)}, bf16[128,256]{1,0:T(8,128)(2,1)S(1)}, u32[]{:S(2)}, u32[]{:S(2)}) collective-permute-start(bf16[128,256]{1,0:T(8,128)(2,1)S(1)} %get-tuple-element.48), channel_id=1, source_target_pairs={{2,0},{6,4},{10,8},{14,12},{18,16},{22,20},{26,24},{30,28},{0,2},{... | collective-permute-start | bytes 196616 | tf_op jit(solution)/shard_map/ppermute | solution.py:277
  18.5 4.6 %collective-permute-start.6 = (bf16[128,256]{1,0:T(8,128)(2,1)S(1)}, bf16[128,256]{1,0:T(8,128)(2,1)S(1)}, u32[]{:S(2)}, u32[]{:S(2)}) collective-permute-start(bf16[128,256]{1,0:T(8,128)(2,1)S(1)} %get-tuple-element.50), channel_id=1, source_target_pairs={{0,1},{1,0},{2,3},{3,2},{4,5},{5,4},{6,7},{7,6},{8,9},{9,8},{10,11... | collective-permute-start | bytes 196616 | tf_op jit(solution)/shard_map/ppermute | solution.py:307
